TPU v7x, 128 devices: a whole 4x4x4 slice. The times are simulated.
128 devices in a mesh: dp: 4 (over z), seq: 4 (over y), tensor: 8 (over x, core).
Axes of the slice: x: 4, y: 4, z: 4, core: 2. Of those that a mesh axis runs over, the one named last changes fastest.
Arguments:
- activations: bfloat16 [12, 352, 8192], P('dp', 'seq', 'tensor'), may hold values from -6 to 6
- cotangents: bfloat16 [12, 352, 14336], P('dp', 'seq', 'tensor'), may hold values from -0.59765625 to 0.59765625
- row_ids: int32 [4, 3], P('dp'), may hold values from 0 to 2, each once within a row
- row_counts: int32 [4, 3], P('dp'), may hold values from 88 to 352
Outputs:
- weighted_grad: float32 [8192, 14336], P(('dp', 'seq'), 'tensor')
- example_weights: float32 [4, 2], P('dp')
All inputs are finite; a program needn't handle non-finite values.
Results may differ from a plain program's by a relative error of at most 0.004.
Values may be sent and summed in bfloat16 or wider, within the bound.
A program may use at most 128 MiB of HBM per device.

v0:
```python
import jax
import jax.numpy as jnp
from jax import lax
from jax.experimental import pallas as pl
from jax.experimental.pallas import tpu as pltpu
from jax.sharding import PartitionSpec as P

MESH = pl.DeviceIdType.MESH
F32 = jnp.float32
BF16 = jnp.bfloat16

SEG = 88
NOISE = 176
CLEAN_ROWS = 96
WA = 768
WB = 1024
LANES = 128


def body_kernel(ids_ref, counts_ref, acts_ref, cot_ref, out_ref, wout_ref,
                na, ca, cg, ga, gb, ao, ata, atb, part_gram, grad_gram, full, d2, sm,
                near_a, near_b, x3, sv1, sv2, wts, scale,
                ring_s, ring_r, p_s, p_r, p_l, k_s, k_r,
                d_s, d_r, m_s, m_r, v_s, v_r):
    z = lax.axis_index("dp")
    y = lax.axis_index("seq")
    t = lax.axis_index("tensor")
    x = t // 2
    c = lax.rem(t, 2)

    def mod4(v):
        return lax.rem(v, 4)

    def copy(src, dst, s, r, dev):
        return pltpu.make_async_remote_copy(
            src_ref=src, dst_ref=dst, send_sem=s, recv_sem=r, device_id=dev, device_id_type=MESH)

    barrier = pltpu.get_barrier_semaphore()

    def greet(dev):
        pl.semaphore_signal(barrier, inc=1, device_id=dev, device_id_type=MESH)

    def cell(r):
        other = lax.rem(4 * z + y + r, 16)
        return other // 4, lax.rem(other, 4), t

    for r in range(1, 16):
        greet(cell(r))
    for r in range(1, 8):
        greet((z, y, lax.rem(t + r, 8)))

    targets = [(h, q, (x, 2 * c + h, 2 * q + z // 2)) for h in range(2) for q in range(4)]
    target_self = [(x == z) & (y == 2 * c + h) & (q == x) & (c == z // 2) for h, q, _ in targets]
    sources = [(2 * c + i // 4, i % 4) for i in range(8)]
    source_self = [(zs == z) & (ys == y) & (x == z) & (c == y // 2) for zs, ys in sources]
    for (_, _, dev), same in zip(targets, target_self):
        @pl.when(jnp.logical_not(same))
        def _():
            greet(dev)
    for (zs, ys), same in zip(sources, source_self):
        @pl.when(jnp.logical_not(same))
        def _():
            greet((zs, ys, 2 * z + y // 2))
    has_self = ((x == z) & (c == y // 2) & (c == z // 2)).astype(jnp.int32)

    rid = [ids_ref[0, j] for j in range(3)]
    live = [counts_ref[0, rid[j]] - y * SEG for j in range(3)]
    rows = lax.broadcasted_iota(jnp.int32, (SEG, LANES), 0)
    pad = jnp.zeros((CLEAN_ROWS - SEG, LANES), F32)

    def stage_acts(i, carry):
        cols = pl.ds(pl.multiple_of(i * LANES, LANES), LANES)
        part = [acts_ref[rid[j], :, cols].astype(F32) for j in range(3)]
        na[y, :, cols] = jnp.concatenate([part[1], part[2]], axis=0).astype(BF16)
        ca[z, :, cols] = jnp.concatenate([part[0], pad], axis=0).astype(BF16)
        return carry

    lax.fori_loop(0, 1024 // LANES, stage_acts, 0)

    def masked(j, cols):
        return jnp.where(rows < live[j], cot_ref[rid[j], :, cols].astype(F32), 0.0)

    def stage_clean(i, carry):
        cols = pl.ds(pl.multiple_of(i * LANES, LANES), LANES)
        cg[z, :, cols] = jnp.concatenate([masked(0, cols), pad], axis=0).astype(BF16)
        return carry

    def stage_a(i, carry):
        cols = pl.ds(pl.multiple_of(i * LANES, LANES), LANES)
        ga[z, y, :, cols] = jnp.concatenate([masked(1, cols), masked(2, cols)], axis=0).astype(BF16)
        return carry

    def stage_b(i, carry):
        cols = pl.ds(pl.multiple_of(i * LANES, LANES), LANES)
        from_cols = pl.ds(pl.multiple_of(WA + i * LANES, LANES), LANES)
        gb[y, z, :, cols] = jnp.concatenate(
            [masked(1, from_cols), masked(2, from_cols)], axis=0).astype(BF16)
        return carry

    pl.semaphore_wait(barrier, 38 - 2 * has_self)

    pieces = []
    for i, ((h, q, dev), same) in enumerate(zip(targets, target_self)):
        src = na.at[y, :, pl.ds(h * 512 + q * LANES, LANES)]
        dst = ao.at[q, z, y]
        far_copy = copy(src, dst, p_s.at[i], p_r.at[lax.rem(z, 2) * 4 + y], dev)
        near_copy = pltpu.make_async_copy(src, dst, p_l)

        @pl.when(same)
        def _():
            near_copy.start()

        @pl.when(jnp.logical_not(same))
        def _():
            far_copy.start()
        pieces.append((far_copy, near_copy, same))

    rings = []

    class Ring:
        def __init__(self, at, axis, first, second):
            n = len(rings)
            rings.append(self)
            me = {"x": x, "y": y, "z": z}[axis]

            def dev(v):
                return {"x": (z, y, 2 * v + c), "y": (z, v, t), "z": (v, y, t)}[axis]

            up, down, far = mod4(me + 1), mod4(me + 3), mod4(me + 2)
            own, low, high, opp = at(me), at(down), at(up), at(far)
            self.go = [copy(own, own, ring_s.at[n, 0], ring_r.at[n, 0], dev(up)),
                       copy(own, own, ring_s.at[n, 1], ring_r.at[n, 1], dev(down))]
            self.got = [copy(low, low, ring_s.at[n, 0], ring_r.at[n, 0], dev(up)),
                        copy(high, high, ring_s.at[n, 1], ring_r.at[n, 1], dev(down))]
            self.pass_on = [
                copy(low.at[first], low.at[first], ring_s.at[n, 2], ring_r.at[n, 2], dev(up)),
                copy(high.at[second], high.at[second], ring_s.at[n, 3], ring_r.at[n, 3], dev(down))]
            self.got_far = [
                copy(opp.at[first], opp.at[first], ring_s.at[n, 2], ring_r.at[n, 2], dev(up)),
                copy(opp.at[second], opp.at[second], ring_s.at[n, 3], ring_r.at[n, 3], dev(down))]

        def start(self):
            for k in self.go:
                k.start()

        def forward(self):
            for k in range(2):
                self.got[k].wait_recv()
                self.pass_on[k].start()

        def finish(self):
            for k in self.got_far:
                k.wait_recv()

        def drain(self):
            for k in self.go + self.pass_on:
                k.wait_send()

    def halves(width):
        half = width // 2
        return (slice(None), pl.ds(0, half)), (slice(None), pl.ds(half, half))

    def az_ring(k):
        item = mod4(y + k)
        return Ring(lambda v: ga.at[v, item], "z", *halves(WA))

    def by_ring(k):
        item = mod4(z + k)
        return Ring(lambda v: gb.at[v, item], "y", *halves(WB))

    def rows_of(chunk):
        return pl.ds(pl.multiple_of(chunk * SEG, 8), SEG)

    r_na = Ring(lambda v: na.at[v], "y", *halves(1024))
    r_ca = Ring(lambda v: ca.at[v], "z", *halves(1024))
    r_cg = Ring(lambda v: cg.at[v], "z", *halves(WA + WB))
    r_ay = Ring(lambda v: ga.at[z, v], "y", *halves(WA))
    r_bz = Ring(lambda v: gb.at[y, v], "z", *halves(WB))
    r_az = {k: az_ring(k) for k in (0, 3, 1, 2)}
    r_by = {k: by_ring(k) for k in (0, 3, 1, 2)}
    here = pl.ds(2 * c, 2)
    there = pl.ds(2 * (1 - c), 2)
    r_ao = Ring(lambda v: ao.at[v, here], "x", (pl.ds(0, 1),), (pl.ds(1, 1),))
    r_full = Ring(lambda v: full.at[rows_of(4 * c + v)], "x", (pl.ds(0, 48),), (pl.ds(48, 40),))

    r_na.start()
    r_ca.start()
    lax.fori_loop(0, WA // LANES, stage_a, 0)
    r_ay.start()
    lax.fori_loop(0, (WA + WB) // LANES, stage_clean, 0)
    r_cg.start()
    lax.fori_loop(0, WB // LANES, stage_b, 0)
    r_bz.start()

    r_na.forward()
    r_by[0].start()
    for i, ((zs, ys), same) in enumerate(zip(sources, source_self)):
        dst = ao.at[x, zs, ys]
        far_copy = copy(dst, dst, p_s.at[i], p_r.at[i], (z, y, lax.rem(t + 1, 8)))
        near_copy = pltpu.make_async_copy(dst, dst, p_l)

        @pl.when(same)
        def _():
            near_copy.wait()

        @pl.when(jnp.logical_not(same))
        def _():
            far_copy.wait_recv()
    mine = ao.at[x, here]
    partner = (z, y, 2 * x + 1 - c)
    r_ao.start()
    core = [copy(mine, mine, k_s.at[0], k_r.at[0], partner)]
    core[0].start()

    r_ca.forward()
    r_cg.forward()
    r_az[0].start()
    r_ay.forward()
    r_az[3].start()
    r_az[1].start()
    r_bz.forward()

    def relay(r):
        block = ao.at[mod4(x + 4 - r), here]
        core.append(copy(block, block, k_s.at[r], k_r.at[r], partner))
        core[-1].start()

    r_ao.forward()
    relay(1)
    relay(3)

    contract = (((1,), (1,)), ((), ()))

    def gram(left, right):
        return lax.dot_general(left, right, contract, preferred_element_type=F32)

    r_na.finish()
    r_ca.finish()
    part_gram[...] = gram(na[...].reshape(4 * NOISE, 1024), ca[...].reshape(4 * CLEAN_ROWS, 1024))
    own_half = pl.ds(pl.multiple_of(c * 352, 8), 352)
    other_half = pl.ds(pl.multiple_of((1 - c) * 352, 8), 352)
    swap = copy(part_gram.at[other_half], d2, d_s.at[0], d_r.at[0], partner)
    swap.start()

    r_by[0].forward()
    r_by[3].start()
    r_by[1].start()
    r_ao.finish()
    relay(2)

    swap.wait_recv()
    sm[...] = part_gram[own_half] + d2[...]
    up, down, across = mod4(x + 1), mod4(x + 3), mod4(x + 2)
    dev_up, dev_down = (z, y, 2 * up + c), (z, y, 2 * down + c)
    first = pl.ds(pl.multiple_of(across * SEG, 8), 48)
    second = pl.ds(pl.multiple_of(across * SEG + 48, 8), 40)
    share = [copy(sm.at[first], near_a, m_s.at[0], m_r.at[0], dev_up),
             copy(sm.at[second], near_b, m_s.at[1], m_r.at[1], dev_down),
             copy(sm.at[rows_of(up)], x3.at[0], m_s.at[2], m_r.at[2], dev_up),
             copy(sm.at[rows_of(down)], x3.at[1], m_s.at[3], m_r.at[3], dev_down)]
    share[0].start()
    share[1].start()
    r_az[0].forward()
    share[0].wait_recv()
    sm[pl.ds(pl.multiple_of(up * SEG, 8), 48)] += near_a[...]
    share[2].start()
    share[1].wait_recv()
    sm[pl.ds(pl.multiple_of(down * SEG + 48, 8), 40)] += near_b[...]
    share[3].start()

    r_cg.finish()
    r_ay.finish()
    r_az[2].start()
    grad_gram[...] = gram(ga[z].reshape(4 * NOISE, WA), cg[:, :, :WA].reshape(4 * CLEAN_ROWS, WA))

    share[2].wait_recv()
    share[3].wait_recv()
    full[rows_of(4 * c + x)] = sm[rows_of(x)] + x3[0] + x3[1]
    r_full.start()
    r_bz.finish()
    r_by[2].start()
    r_full.forward()
    r_full.finish()
    give = copy(full.at[own_half], full.at[own_half], d_s.at[1], d_r.at[1], partner)
    give.start()

    r_by[0].finish()
    grad_gram[...] += gram(gb[:, z].reshape(4 * NOISE, WB), cg[:, :, WA:].reshape(4 * CLEAN_ROWS, WB))
    copy(full.at[other_half], full.at[other_half], d_s.at[1], d_r.at[1], partner).wait_recv()

    def row_dot(j):
        terms = [grad_gram[g * SEG:(g + 1) * SEG] * full[g * SEG:(g + 1) * SEG] for g in range(j, 8, 2)]
        rows_sum = jnp.sum(terms[0] + terms[1] + terms[2] + terms[3], axis=0, keepdims=True)
        return jnp.broadcast_to(jnp.sum(rows_sum, axis=1, keepdims=True), (8, LANES))

    place = lax.broadcasted_iota(jnp.int32, (8, LANES), 0)
    tile = jnp.where(place == 2 * z, row_dot(0), jnp.where(place == 2 * z + 1, row_dot(1), 0.0))

    sends = []

    def send_tile(buf, value, me, n, dev, base):
        buf[me] = value
        for r in range(1, n):
            out = copy(buf.at[me], buf.at[me], v_s.at[base + r], v_r.at[base + r], dev(r))
            out.start()
            sends.append(out)

    def sum_tiles(buf, me, n, base):
        for r in range(1, n):
            origin = buf.at[lax.rem(me + n - r, n)]
            copy(origin, origin, v_s.at[base + r], v_r.at[base + r], partner).wait_recv()
        return jnp.sum(buf[...], axis=0)

    send_tile(sv1, tile, t, 8, lambda r: (z, y, lax.rem(t + r, 8)), 0)

    for r in range(4):
        block = ao.at[mod4(x + 4 - r), there]
        copy(block, block, k_s.at[r], k_r.at[r], partner).wait_recv()

    def turn(k, carry):
        for q in range(4):
            span = pl.ds(q * LANES, LANES)
            ata[k, span, :] = ao[q, k].reshape(4 * NOISE, LANES).T
            atb[k, span, :] = ao[q, :, k].reshape(4 * NOISE, LANES).T
        return carry

    lax.fori_loop(0, 4, turn, 0)

    tile = sum_tiles(sv1, t, 8, 0)
    send_tile(sv2, tile, 4 * z + y, 16, cell, 8)
    for k in (3, 1):
        r_az[k].forward()
        r_by[k].forward()
    r_az[2].forward()
    r_by[2].forward()
    tile = sum_tiles(sv2, 4 * z + y, 16, 8)
    weights = jnp.maximum(-tile, 0.0) / jnp.sum(jnp.abs(tile), axis=0, keepdims=True)
    wts[...] = weights
    for k in range(4):
        scale[k, :SEG] = jnp.broadcast_to(wts[2 * k:2 * k + 1, :], (SEG, LANES))
        scale[k, SEG:] = jnp.broadcast_to(wts[2 * k + 1:2 * k + 2, :], (SEG, LANES))
    lane = lax.broadcasted_iota(jnp.int32, (1, LANES), 1)
    wout_ref[...] = jnp.where(lane == 0, wts[pl.ds(2 * z, 1), :], wts[pl.ds(2 * z + 1, 1), :])[:, :2]

    def scaled(raw, s):
        full = jnp.concatenate([s, s], axis=1)
        return (raw.astype(F32) * full).astype(BF16)

    def product(at, pieces_of, width, base, first):
        def step(i, carry):
            cols = pl.ds(pl.multiple_of(i * 256, 256), 256)
            dest = pl.ds(pl.multiple_of(base + i * 256, 256), 256)
            right = jnp.concatenate([scaled(raw, s) for raw, s in pieces_of(cols)], axis=0)
            value = jnp.dot(at[...], right, preferred_element_type=F32)
            if first:
                out_ref[:, dest] = value
            else:
                out_ref[:, dest] += value
            return carry

        lax.fori_loop(0, width // 256, step, 0)

    def add_a(k, first=False):
        v = mod4(z + k)
        product(ata.at[v], lambda cols: [(ga[v, i, :, cols], scale[v]) for i in range(4)], WA, 0, first)

    def add_b(k, first=False):
        v = mod4(y + k)
        product(atb.at[v], lambda cols: [(gb[v, i, :, cols], scale[i]) for i in range(4)], WB, WA, first)

    add_a(0, True)
    add_b(0, True)
    for k in (3, 1):
        add_a(k)
        add_b(k)
    for k in (0, 3, 1, 2):
        r_az[k].finish()
    add_a(2)
    for k in (3, 1, 2):
        r_by[k].finish()
    add_b(2)

    for far_copy, _, same in pieces:
        @pl.when(jnp.logical_not(same))
        def _():
            far_copy.wait_send()
    for ring in rings:
        ring.drain()
    for k in core + [swap, give] + share + sends:
        k.wait_send()


def body(activations, cotangents, row_ids, row_counts):
    dma = pltpu.SemaphoreType.DMA
    vmem = pltpu.VMEM
    return pl.pallas_call(
        body_kernel,
        out_shape=(pltpu.VMEM((512, WA + WB), F32), pltpu.VMEM((1, 2), F32)),
        in_specs=[pl.BlockSpec(memory_space=pltpu.SMEM)] * 2 + [pl.BlockSpec(memory_space=pltpu.VMEM)] * 2,
        out_specs=(pl.BlockSpec(memory_space=pltpu.VMEM), pl.BlockSpec(memory_space=pltpu.VMEM)),
        scratch_shapes=[
            vmem((4, NOISE, 1024), BF16),
            vmem((4, CLEAN_ROWS, 1024), BF16),
            vmem((4, CLEAN_ROWS, WA + WB), BF16),
            vmem((4, 4, NOISE, WA), BF16),
            vmem((4, 4, NOISE, WB), BF16),
            vmem((4, 4, 4, NOISE, LANES), BF16),
            vmem((4, 512, 4 * NOISE), BF16),
            vmem((4, 512, 4 * NOISE), BF16),
            vmem((4 * NOISE, 4 * CLEAN_ROWS), F32),
            vmem((4 * NOISE, 4 * CLEAN_ROWS), F32),
            vmem((4 * NOISE, 4 * CLEAN_ROWS), F32),
            vmem((2 * NOISE, 4 * CLEAN_ROWS), F32),
            vmem((2 * NOISE, 4 * CLEAN_ROWS), F32),
            vmem((48, 4 * CLEAN_ROWS), F32),
            vmem((40, 4 * CLEAN_ROWS), F32),
            vmem((2, SEG, 4 * CLEAN_ROWS), F32),
            vmem((8, 8, LANES), F32),
            vmem((16, 8, LANES), F32),
            vmem((8, LANES), F32),
            vmem((4, NOISE, LANES), F32),
            dma((15, 4)), dma((15, 4)),
            dma((8,)), dma((8,)), dma,
            dma((4,)), dma((4,)),
            dma((2,)), dma((2,)),
            dma((4,)), dma((4,)),
            dma((24,)), dma((24,)),
        ],
        compiler_params=pltpu.CompilerParams(
            collective_id=0, has_side_effects=True, vmem_limit_bytes=60 * 1024 * 1024),
        cost_estimate=pl.CostEstimate(flops=8_000_000_000, bytes_accessed=8_000_000, transcendentals=0),
        name="reweight",
    )(row_ids, row_counts, activations, cotangents)


def solution(mesh):
    placed = (P("dp", "seq", "tensor"), P("dp", "seq", "tensor"), P("dp", None), P("dp", None))
    return jax.shard_map(
        body,
        mesh=mesh,
        in_specs=placed,
        out_specs=(P(("dp", "seq"), "tensor"), P("dp", None)),
        check_vma=False,
    )
```

profile of v0, /device:TPU:0, one launch (start us, length us, event | category | flops | bytes accessed | tf_op | source)
XLA Modules:
  0.0 92.0 jit_solution(724375312902199575)
XLA Ops:
  0.6 89.0 %reweight.1 = (f32[512,1792]{1,0:T(8,128)S(1)}, f32[1,2]{1,0:T(1,128)S(1)}) custom-call(s32[1,3]{1,0:T(1,128)} %ids_ref.1, s32[1,3]{1,0:T(1,128)} %counts_ref.1, bf16[3,88,1024]{2,1,0:T(8,128)(2,1)} %acts_ref.1, bf16[3,88,1792]{2,1,0:T(8,128)(2,1)} %cot_ref.1), custom_call_target="tpu_custom_call" | custom-call | flops 8000000000 | bytes 8000000 | tf_op jit(solution)/shard_map/reweight/pallas_call | solution.py:396
  89.6 1.8 %copy.8 = f32[512,1792]{1,0:T(8,128)} copy(f32[512,1792]{1,0:T(8,128)S(1)} %get-tuple-element.2) | data formatting | bytes 7340032
  91.5 0.5 copy.9
where the time goes:
time: 92.5 us; the launch traced here: 92 us
  Pallas kernels  89 us (96%)
  local copies, waits for them, and re-layouts  2.35 us (3%)
    pallas_call x1, Pallas kernels, body(): pl.pallas_call(body_kernel, out_shape=(pltpu.VMEM((512, WA + WB), F32), p...  89 us
    unnamed x2, local copies, waits for them, and re-layouts  2.35 us

commit v1 on v0

--- a/solution.py
+++ b/solution.py
@@ -190,8 +190,9 @@
     lax.fori_loop(0, (WA + WB) // LANES, stage_clean, 0)
     r_cg.start()
     lax.fori_loop(0, WB // LANES, stage_b, 0)
+
+    r_ca.forward()
     r_bz.start()
-
     r_na.forward()
     r_by[0].start()
     for i, ((zs, ys), same) in enumerate(zip(sources, source_self)):
@@ -212,22 +213,14 @@
     core = [copy(mine, mine, k_s.at[0], k_r.at[0], partner)]
     core[0].start()
 
-    r_ca.forward()
-    r_cg.forward()
-    r_az[0].start()
-    r_ay.forward()
-    r_az[3].start()
-    r_az[1].start()
-    r_bz.forward()
-
     def relay(r):
         block = ao.at[mod4(x + 4 - r), here]
         core.append(copy(block, block, k_s.at[r], k_r.at[r], partner))
         core[-1].start()
 
-    r_ao.forward()
-    relay(1)
-    relay(3)
+    r_cg.forward()
+    r_az[0].start()
+    r_ay.forward()
 
     contract = (((1,), (1,)), ((), ()))
 
@@ -242,11 +235,12 @@
     swap = copy(part_gram.at[other_half], d2, d_s.at[0], d_r.at[0], partner)
     swap.start()
 
-    r_by[0].forward()
-    r_by[3].start()
-    r_by[1].start()
-    r_ao.finish()
-    relay(2)
+    r_ao.forward()
+    relay(1)
+    relay(3)
+    r_bz.forward()
+    r_az[3].start()
+    r_az[1].start()
 
     swap.wait_recv()
     sm[...] = part_gram[own_half] + d2[...]
@@ -260,7 +254,11 @@
              copy(sm.at[rows_of(down)], x3.at[1], m_s.at[3], m_r.at[3], dev_down)]
     share[0].start()
     share[1].start()
-    r_az[0].forward()
+    r_ao.finish()
+    relay(2)
+    r_by[0].forward()
+    r_by[3].start()
+    r_by[1].start()
     share[0].wait_recv()
     sm[pl.ds(pl.multiple_of(up * SEG, 8), 48)] += near_a[...]
     share[2].start()
@@ -277,13 +275,14 @@
     share[3].wait_recv()
     full[rows_of(4 * c + x)] = sm[rows_of(x)] + x3[0] + x3[1]
     r_full.start()
-    r_bz.finish()
-    r_by[2].start()
+    r_az[0].forward()
     r_full.forward()
     r_full.finish()
     give = copy(full.at[own_half], full.at[own_half], d_s.at[1], d_r.at[1], partner)
     give.start()
 
+    r_bz.finish()
+    r_by[2].start()
     r_by[0].finish()
     grad_gram[...] += gram(gb[:, z].reshape(4 * NOISE, WB), cg[:, :, WA:].reshape(4 * CLEAN_ROWS, WB))
     copy(full.at[other_half], full.at[other_half], d_s.at[1], d_r.at[1], partner).wait_recv()
@@ -328,11 +327,8 @@
 
     tile = sum_tiles(sv1, t, 8, 0)
     send_tile(sv2, tile, 4 * z + y, 16, cell, 8)
-    for k in (3, 1):
-        r_az[k].forward()
-        r_by[k].forward()
-    r_az[2].forward()
-    r_by[2].forward()
+    r_az[3].forward()
+    r_by[3].forward()
     tile = sum_tiles(sv2, 4 * z + y, 16, 8)
     weights = jnp.maximum(-tile, 0.0) / jnp.sum(jnp.abs(tile), axis=0, keepdims=True)
     wts[...] = weights
@@ -369,10 +365,15 @@
         product(atb.at[v], lambda cols: [(gb[v, i, :, cols], scale[i]) for i in range(4)], WB, WA, first)
 
     add_a(0, True)
+    r_az[1].forward()
+    r_by[1].forward()
     add_b(0, True)
-    for k in (3, 1):
-        add_a(k)
-        add_b(k)
+    r_az[2].forward()
+    add_a(3)
+    r_by[2].forward()
+    add_a(1)
+    add_b(3)
+    add_b(1)
     for k in (0, 3, 1, 2):
         r_az[k].finish()
     add_a(2)

time: 92.5 us -> 91.7 us (level)
  no operation moved by 1% of the time
where the time goes in v1:
time: 91.7 us; the launch traced here: 91.1 us
  Pallas kernels  88.1 us (96%)
  local copies, waits for them, and re-layouts  2.35 us (3%)
    pallas_call x1, Pallas kernels, body(): pl.pallas_call(body_kernel, out_shape=(pltpu.VMEM((512, WA + WB), F32), p...  88.1 us
    unnamed x2, local copies, waits for them, and re-layouts  2.35 us

profile of v1, /device:TPU:0, one launch (start us, length us, event | category | flops | bytes accessed | tf_op | source)
XLA Modules:
  0.0 91.1 jit_solution(7036058576811153508)
XLA Ops:
  0.6 88.1 %reweight.1 = (f32[512,1792]{1,0:T(8,128)S(1)}, f32[1,2]{1,0:T(1,128)S(1)}) custom-call(s32[1,3]{1,0:T(1,128)} %ids_ref.1, s32[1,3]{1,0:T(1,128)} %counts_ref.1, bf16[3,88,1024]{2,1,0:T(8,128)(2,1)} %acts_ref.1, bf16[3,88,1792]{2,1,0:T(8,128)(2,1)} %cot_ref.1), custom_call_target="tpu_custom_call" | custom-call | flops 8000000000 | bytes 8000000 | tf_op jit(solution)/shard_map/reweight/pallas_call | solution.py:397
  88.8 1.8 %copy.8 = f32[512,1792]{1,0:T(8,128)} copy(f32[512,1792]{1,0:T(8,128)S(1)} %get-tuple-element.2) | data formatting | bytes 7340032
  90.6 0.5 copy.9

commit v2 on v1

--- a/solution.py
+++ b/solution.py
@@ -156,26 +156,26 @@
             for k in self.go + self.pass_on:
                 k.wait_send()
 
-    def halves(width):
-        half = width // 2
-        return (slice(None), pl.ds(0, half)), (slice(None), pl.ds(half, half))
+    even = (pl.ds(0, 96),), (pl.ds(96, 80),)
+    odd = (pl.ds(80, 96),), (pl.ds(0, 80),)
+    equal = (pl.ds(0, 48),), (pl.ds(48, 48),)
 
     def az_ring(k):
         item = mod4(y + k)
-        return Ring(lambda v: ga.at[v, item], "z", *halves(WA))
+        return Ring(lambda v: ga.at[v, item], "z", *(even if k in (0, 1) else odd))
 
     def by_ring(k):
         item = mod4(z + k)
-        return Ring(lambda v: gb.at[v, item], "y", *halves(WB))
+        return Ring(lambda v: gb.at[v, item], "y", *(even if k in (0, 1) else odd))
 
     def rows_of(chunk):
         return pl.ds(pl.multiple_of(chunk * SEG, 8), SEG)
 
-    r_na = Ring(lambda v: na.at[v], "y", *halves(1024))
-    r_ca = Ring(lambda v: ca.at[v], "z", *halves(1024))
-    r_cg = Ring(lambda v: cg.at[v], "z", *halves(WA + WB))
-    r_ay = Ring(lambda v: ga.at[z, v], "y", *halves(WA))
-    r_bz = Ring(lambda v: gb.at[y, v], "z", *halves(WB))
+    r_na = Ring(lambda v: na.at[v], "y", *even)
+    r_ca = Ring(lambda v: ca.at[v], "z", *equal)
+    r_cg = Ring(lambda v: cg.at[v], "z", *equal)
+    r_ay = Ring(lambda v: ga.at[z, v], "y", *odd)
+    r_bz = Ring(lambda v: gb.at[y, v], "z", *odd)
     r_az = {k: az_ring(k) for k in (0, 3, 1, 2)}
     r_by = {k: by_ring(k) for k in (0, 3, 1, 2)}
     here = pl.ds(2 * c, 2)

time: 91.7 us -> 91.8 us (level)
  no operation moved by 1% of the time
where the time goes in v2:
time: 91.8 us; the launch traced here: 91.7 us
  Pallas kernels  88.7 us (97%)
  local copies, waits for them, and re-layouts  2.35 us (3%)
    pallas_call x1, Pallas kernels, body(): pl.pallas_call(body_kernel, out_shape=(pltpu.VMEM((512, WA + WB), F32), p...  88.7 us
    unnamed x2, local copies, waits for them, and re-layouts  2.35 us

profile of v2, /device:TPU:0, one launch (start us, length us, event | category | flops | bytes accessed | tf_op | source)
XLA Modules:
  0.0 91.7 jit_solution(9212188723470538543)
XLA Ops:
  0.6 88.7 %reweight.1 = (f32[512,1792]{1,0:T(8,128)S(1)}, f32[1,2]{1,0:T(1,128)S(1)}) custom-call(s32[1,3]{1,0:T(1,128)} %ids_ref.1, s32[1,3]{1,0:T(1,128)} %counts_ref.1, bf16[3,88,1024]{2,1,0:T(8,128)(2,1)} %acts_ref.1, bf16[3,88,1792]{2,1,0:T(8,128)(2,1)} %cot_ref.1), custom_call_target="tpu_custom_call" | custom-call | flops 8000000000 | bytes 8000000 | tf_op jit(solution)/shard_map/reweight/pallas_call | solution.py:397
  89.3 1.8 %copy.8 = f32[512,1792]{1,0:T(8,128)} copy(f32[512,1792]{1,0:T(8,128)S(1)} %get-tuple-element.2) | data formatting | bytes 7340032
  91.2 0.5 copy.9

commit v3 on v2

--- a/solution.py
+++ b/solution.py
@@ -18,9 +18,9 @@
 
 
 def body_kernel(ids_ref, counts_ref, acts_ref, cot_ref, out_ref, wout_ref,
-                na, ca, cg, ga, gb, ao, ata, atb, part_gram, grad_gram, full, d2, sm,
+                na, ca, cg, ga, gb, hop, ao, ata, atb, part_gram, grad_gram, full, d2, sm,
                 near_a, near_b, x3, sv1, sv2, wts, scale,
-                ring_s, ring_r, p_s, p_r, p_l, k_s, k_r,
+                ring_s, ring_r, h_s, h_r, p_s, p_r, p_l, k_s, k_r,
                 d_s, d_r, m_s, m_r, v_s, v_r):
     z = lax.axis_index("dp")
     y = lax.axis_index("seq")
@@ -49,10 +49,10 @@
     for r in range(1, 8):
         greet((z, y, lax.rem(t + r, 8)))
 
-    targets = [(h, q, (x, 2 * c + h, 2 * q + z // 2)) for h in range(2) for q in range(4)]
-    target_self = [(x == z) & (y == 2 * c + h) & (q == x) & (c == z // 2) for h, q, _ in targets]
+    targets = [(r, h, (mod4(x + r), 2 * c + h, 2 * x + z // 2)) for r in range(4) for h in range(2)]
+    target_self = [(dev[0] == z) & (dev[1] == y) & (c == z // 2) for _, _, dev in targets]
     sources = [(2 * c + i // 4, i % 4) for i in range(8)]
-    source_self = [(zs == z) & (ys == y) & (x == z) & (c == y // 2) for zs, ys in sources]
+    source_self = [(zs == z) & (ys == y) & (c == y // 2) for zs, ys in sources]
     for (_, _, dev), same in zip(targets, target_self):
         @pl.when(jnp.logical_not(same))
         def _():
@@ -60,8 +60,8 @@
     for (zs, ys), same in zip(sources, source_self):
         @pl.when(jnp.logical_not(same))
         def _():
-            greet((zs, ys, 2 * z + y // 2))
-    has_self = ((x == z) & (c == y // 2) & (c == z // 2)).astype(jnp.int32)
+            greet((zs, ys, 2 * x + y // 2))
+    has_self = ((c == y // 2) & (c == z // 2)).astype(jnp.int32)
 
     rid = [ids_ref[0, j] for j in range(3)]
     live = [counts_ref[0, rid[j]] - y * SEG for j in range(3)]
@@ -99,10 +99,26 @@
 
     pl.semaphore_wait(barrier, 38 - 2 * has_self)
 
+    hops = []
+    for r in range(1, 4):
+        q = mod4(x + r)
+        for h in range(2):
+            src = na.at[y, :, pl.ds(pl.multiple_of(h * 512 + q * LANES, LANES), LANES)]
+            hops.append(copy(src, hop.at[r, h], h_s.at[r, h], h_r.at[r, h], (z, y, 2 * q + c)))
+    for k in hops:
+        k.start()
+
     pieces = []
-    for i, ((h, q, dev), same) in enumerate(zip(targets, target_self)):
-        src = na.at[y, :, pl.ds(h * 512 + q * LANES, LANES)]
-        dst = ao.at[q, z, y]
+
+    def send_piece(i):
+        r, h, dev = targets[i]
+        same = target_self[i]
+        if r:
+            src = hop.at[4 - r, h]
+            copy(src, src, h_s.at[4 - r, h], h_r.at[4 - r, h], (z, y, lax.rem(t + 1, 8))).wait_recv()
+        else:
+            src = na.at[y, :, pl.ds(pl.multiple_of(h * 512 + x * LANES, LANES), LANES)]
+        dst = ao.at[x, z, y]
         far_copy = copy(src, dst, p_s.at[i], p_r.at[lax.rem(z, 2) * 4 + y], dev)
         near_copy = pltpu.make_async_copy(src, dst, p_l)
 
@@ -113,7 +129,7 @@
         @pl.when(jnp.logical_not(same))
         def _():
             far_copy.start()
-        pieces.append((far_copy, near_copy, same))
+        pieces.append((far_copy, same))
 
     rings = []
 
@@ -191,10 +207,18 @@
     r_cg.start()
     lax.fori_loop(0, WB // LANES, stage_b, 0)
 
+    send_piece(0)
+    send_piece(1)
     r_ca.forward()
     r_bz.start()
     r_na.forward()
     r_by[0].start()
+    for i in range(2, 8):
+        send_piece(i)
+    r_cg.forward()
+    r_az[0].start()
+    r_ay.forward()
+
     for i, ((zs, ys), same) in enumerate(zip(sources, source_self)):
         dst = ao.at[x, zs, ys]
         far_copy = copy(dst, dst, p_s.at[i], p_r.at[i], (z, y, lax.rem(t + 1, 8)))
@@ -217,10 +241,6 @@
         block = ao.at[mod4(x + 4 - r), here]
         core.append(copy(block, block, k_s.at[r], k_r.at[r], partner))
         core[-1].start()
-
-    r_cg.forward()
-    r_az[0].start()
-    r_ay.forward()
 
     contract = (((1,), (1,)), ((), ()))
 
@@ -235,9 +255,6 @@
     swap = copy(part_gram.at[other_half], d2, d_s.at[0], d_r.at[0], partner)
     swap.start()
 
-    r_ao.forward()
-    relay(1)
-    relay(3)
     r_bz.forward()
     r_az[3].start()
     r_az[1].start()
@@ -254,8 +271,9 @@
              copy(sm.at[rows_of(down)], x3.at[1], m_s.at[3], m_r.at[3], dev_down)]
     share[0].start()
     share[1].start()
-    r_ao.finish()
-    relay(2)
+    r_ao.forward()
+    relay(1)
+    relay(3)
     r_by[0].forward()
     r_by[3].start()
     r_by[1].start()
@@ -277,6 +295,8 @@
     r_full.start()
     r_az[0].forward()
     r_full.forward()
+    r_ao.finish()
+    relay(2)
     r_full.finish()
     give = copy(full.at[own_half], full.at[own_half], d_s.at[1], d_r.at[1], partner)
     give.start()
@@ -381,13 +401,13 @@
         r_by[k].finish()
     add_b(2)
 
-    for far_copy, _, same in pieces:
+    for far_copy, same in pieces:
         @pl.when(jnp.logical_not(same))
         def _():
             far_copy.wait_send()
     for ring in rings:
         ring.drain()
-    for k in core + [swap, give] + share + sends:
+    for k in hops + core + [swap, give] + share + sends:
         k.wait_send()
 
 
@@ -405,6 +425,7 @@
             vmem((4, CLEAN_ROWS, WA + WB), BF16),
             vmem((4, 4, NOISE, WA), BF16),
             vmem((4, 4, NOISE, WB), BF16),
+            vmem((4, 2, NOISE, LANES), BF16),
             vmem((4, 4, 4, NOISE, LANES), BF16),
             vmem((4, 512, 4 * NOISE), BF16),
             vmem((4, 512, 4 * NOISE), BF16),
@@ -421,6 +442,7 @@
             vmem((8, LANES), F32),
             vmem((4, NOISE, LANES), F32),
             dma((15, 4)), dma((15, 4)),
+            dma((4, 2)), dma((4, 2)),
             dma((8,)), dma((8,)), dma,
             dma((4,)), dma((4,)),
             dma((2,)), dma((2,)),

time: 91.8 us -> 102 us (1.11)
  Pallas kernels: 88.7 us -> 98.5 us
    pallas_call x1, Pallas kernels: 88.7 us -> 98.5 us  [body(): pl.pallas_call(body_kernel, out_shape=(pltpu.VMEM((512, WA + WB), F32), p...]
where the time goes in v3:
time: 102 us
  Pallas kernels  98.5 us (97%)
  local copies, waits for them, and re-layouts  2.35 us (2%)
    pallas_call x1, Pallas kernels, body(): pl.pallas_call(body_kernel, out_shape=(pltpu.VMEM((512, WA + WB), F32), p...  98.5 us
    unnamed x2, local copies, waits for them, and re-layouts  2.35 us

profile of v3, /device:TPU:0, one launch (start us, length us, event | category | flops | bytes accessed | tf_op | source)
XLA Modules:
  0.0 101.5 jit_solution(4766198550026534748)
XLA Ops:
  0.6 98.5 %reweight.1 = (f32[512,1792]{1,0:T(8,128)S(1)}, f32[1,2]{1,0:T(1,128)S(1)}) custom-call(s32[1,3]{1,0:T(1,128)} %ids_ref.1, s32[1,3]{1,0:T(1,128)} %counts_ref.1, bf16[3,88,1024]{2,1,0:T(8,128)(2,1)} %acts_ref.1, bf16[3,88,1792]{2,1,0:T(8,128)(2,1)} %cot_ref.1), custom_call_target="tpu_custom_call" | custom-call | flops 8000000000 | bytes 8000000 | tf_op jit(solution)/shard_map/reweight/pallas_call | solution.py:417
  99.2 1.8 %copy.8 = f32[512,1792]{1,0:T(8,128)} copy(f32[512,1792]{1,0:T(8,128)S(1)} %get-tuple-element.2) | data formatting | bytes 7340032
  101.0 0.5 copy.9

commit v4 on v2

--- a/solution.py
+++ b/solution.py
@@ -221,6 +221,9 @@
     r_cg.forward()
     r_az[0].start()
     r_ay.forward()
+    r_ao.forward()
+    relay(1)
+    relay(3)
 
     contract = (((1,), (1,)), ((), ()))
 
@@ -235,12 +238,20 @@
     swap = copy(part_gram.at[other_half], d2, d_s.at[0], d_r.at[0], partner)
     swap.start()
 
-    r_ao.forward()
-    relay(1)
-    relay(3)
+    r_ao.finish()
+    relay(2)
     r_bz.forward()
     r_az[3].start()
     r_az[1].start()
+
+    def turn(k):
+        def step(q, carry):
+            span = pl.ds(pl.multiple_of(q * LANES, LANES), LANES)
+            ata[k, span, :] = ao[q, k].reshape(4 * NOISE, LANES).T
+            atb[k, span, :] = ao[q, :, k].reshape(4 * NOISE, LANES).T
+            return carry
+
+        lax.fori_loop(0, 4, step, 0)
 
     swap.wait_recv()
     sm[...] = part_gram[own_half] + d2[...]
@@ -254,17 +265,20 @@
              copy(sm.at[rows_of(down)], x3.at[1], m_s.at[3], m_r.at[3], dev_down)]
     share[0].start()
     share[1].start()
-    r_ao.finish()
-    relay(2)
+    for r in range(4):
+        block = ao.at[mod4(x + 4 - r), there]
+        copy(block, block, k_s.at[r], k_r.at[r], partner).wait_recv()
     r_by[0].forward()
     r_by[3].start()
     r_by[1].start()
+    turn(0)
     share[0].wait_recv()
     sm[pl.ds(pl.multiple_of(up * SEG, 8), 48)] += near_a[...]
     share[2].start()
     share[1].wait_recv()
     sm[pl.ds(pl.multiple_of(down * SEG + 48, 8), 40)] += near_b[...]
     share[3].start()
+    turn(1)
 
     r_cg.finish()
     r_ay.finish()
@@ -276,7 +290,9 @@
     full[rows_of(4 * c + x)] = sm[rows_of(x)] + x3[0] + x3[1]
     r_full.start()
     r_az[0].forward()
+    turn(2)
     r_full.forward()
+    turn(3)
     r_full.finish()
     give = copy(full.at[own_half], full.at[own_half], d_s.at[1], d_r.at[1], partner)
     give.start()
@@ -311,19 +327,6 @@
         return jnp.sum(buf[...], axis=0)
 
     send_tile(sv1, tile, t, 8, lambda r: (z, y, lax.rem(t + r, 8)), 0)
-
-    for r in range(4):
-        block = ao.at[mod4(x + 4 - r), there]
-        copy(block, block, k_s.at[r], k_r.at[r], partner).wait_recv()
-
-    def turn(k, carry):
-        for q in range(4):
-            span = pl.ds(q * LANES, LANES)
-            ata[k, span, :] = ao[q, k].reshape(4 * NOISE, LANES).T
-            atb[k, span, :] = ao[q, :, k].reshape(4 * NOISE, LANES).T
-        return carry
-
-    lax.fori_loop(0, 4, turn, 0)
 
     tile = sum_tiles(sv1, t, 8, 0)
     send_tile(sv2, tile, 4 * z + y, 16, cell, 8)
@@ -339,13 +342,13 @@
     wout_ref[...] = jnp.where(lane == 0, wts[pl.ds(2 * z, 1), :], wts[pl.ds(2 * z + 1, 1), :])[:, :2]
 
     def scaled(raw, s):
-        full = jnp.concatenate([s, s], axis=1)
+        full = jnp.concatenate([s] * (raw.shape[1] // LANES), axis=1)
         return (raw.astype(F32) * full).astype(BF16)
 
-    def product(at, pieces_of, width, base, first):
+    def product(at, pieces_of, width, base, first, span):
         def step(i, carry):
-            cols = pl.ds(pl.multiple_of(i * 256, 256), 256)
-            dest = pl.ds(pl.multiple_of(base + i * 256, 256), 256)
+            cols = pl.ds(pl.multiple_of(i * span, span), span)
+            dest = pl.ds(pl.multiple_of(base + i * span, 256), span)
             right = jnp.concatenate([scaled(raw, s) for raw, s in pieces_of(cols)], axis=0)
             value = jnp.dot(at[...], right, preferred_element_type=F32)
             if first:
@@ -354,15 +357,15 @@
                 out_ref[:, dest] += value
             return carry
 
-        lax.fori_loop(0, width // 256, step, 0)
+        lax.fori_loop(0, width // span, step, 0)
 
     def add_a(k, first=False):
         v = mod4(z + k)
-        product(ata.at[v], lambda cols: [(ga[v, i, :, cols], scale[v]) for i in range(4)], WA, 0, first)
+        product(ata.at[v], lambda cols: [(ga[v, i, :, cols], scale[v]) for i in range(4)], WA, 0, first, 768)
 
     def add_b(k, first=False):
         v = mod4(y + k)
-        product(atb.at[v], lambda cols: [(gb[v, i, :, cols], scale[i]) for i in range(4)], WB, WA, first)
+        product(atb.at[v], lambda cols: [(gb[v, i, :, cols], scale[i]) for i in range(4)], WB, WA, first, 512)
 
     add_a(0, True)
     r_az[1].forward()

time: 91.8 us -> 91.3 us (level)
  no operation moved by 1% of the time
where the time goes in v4:
time: 91.3 us; the launch traced here: 91.1 us
  Pallas kernels  88.2 us (97%)
  local copies, waits for them, and re-layouts  2.35 us (3%)
    pallas_call x1, Pallas kernels, body(): pl.pallas_call(body_kernel, out_shape=(pltpu.VMEM((512, WA + WB), F32), p...  88.2 us
    unnamed x2, local copies, waits for them, and re-layouts  2.35 us

profile of v4, /device:TPU:0, one launch (start us, length us, event | category | flops | bytes accessed | tf_op | source)
XLA Modules:
  0.0 91.1 jit_solution(5225128565990593162)
XLA Ops:
  0.6 88.2 %reweight.1 = (f32[512,1792]{1,0:T(8,128)S(1)}, f32[1,2]{1,0:T(1,128)S(1)}) custom-call(s32[1,3]{1,0:T(1,128)} %ids_ref.1, s32[1,3]{1,0:T(1,128)} %counts_ref.1, bf16[3,88,1024]{2,1,0:T(8,128)(2,1)} %acts_ref.1, bf16[3,88,1792]{2,1,0:T(8,128)(2,1)} %cot_ref.1), custom_call_target="tpu_custom_call" | custom-call | flops 8000000000 | bytes 8000000 | tf_op jit(solution)/shard_map/reweight/pallas_call | solution.py:400
  88.8 1.8 %copy.8 = f32[512,1792]{1,0:T(8,128)} copy(f32[512,1792]{1,0:T(8,128)S(1)} %get-tuple-element.2) | data formatting | bytes 7340032
  90.6 0.5 copy.9

commit v5 on v4

--- a/solution.py
+++ b/solution.py
@@ -19,7 +19,7 @@
 
 def body_kernel(ids_ref, counts_ref, acts_ref, cot_ref, out_ref, wout_ref,
                 na, ca, cg, ga, gb, ao, ata, atb, part_gram, grad_gram, full, d2, sm,
-                near_a, near_b, x3, sv1, sv2, wts, scale,
+                near_a, near_b, x3, sv1, sv2, wts,
                 ring_s, ring_r, p_s, p_r, p_l, k_s, k_r,
                 d_s, d_r, m_s, m_r, v_s, v_r):
     z = lax.axis_index("dp")
@@ -207,23 +207,12 @@
         @pl.when(jnp.logical_not(same))
         def _():
             far_copy.wait_recv()
-    mine = ao.at[x, here]
     partner = (z, y, 2 * x + 1 - c)
     r_ao.start()
-    core = [copy(mine, mine, k_s.at[0], k_r.at[0], partner)]
-    core[0].start()
-
-    def relay(r):
-        block = ao.at[mod4(x + 4 - r), here]
-        core.append(copy(block, block, k_s.at[r], k_r.at[r], partner))
-        core[-1].start()
-
     r_cg.forward()
     r_az[0].start()
     r_ay.forward()
     r_ao.forward()
-    relay(1)
-    relay(3)
 
     contract = (((1,), (1,)), ((), ()))
 
@@ -239,20 +228,32 @@
     swap.start()
 
     r_ao.finish()
-    relay(2)
     r_bz.forward()
     r_az[3].start()
     r_az[1].start()
 
-    def turn(k):
+    def turn_a(k):
         def step(q, carry):
             span = pl.ds(pl.multiple_of(q * LANES, LANES), LANES)
-            ata[k, span, :] = ao[q, k].reshape(4 * NOISE, LANES).T
-            atb[k, span, :] = ao[q, :, k].reshape(4 * NOISE, LANES).T
+            ata[2 * c + k, span, :] = ao[q, 2 * c + k].reshape(4 * NOISE, LANES).T
             return carry
 
         lax.fori_loop(0, 4, step, 0)
 
+    gap = jnp.zeros((32, LANES), BF16)
+
+    def turn_b(v):
+        def step(q, carry):
+            span = pl.ds(pl.multiple_of(q * LANES, LANES), LANES)
+            tokens = jnp.concatenate([ao[q, 2 * c, v], ao[q, 2 * c + 1, v], gap], axis=0)
+            atb[c, v, span, :] = tokens.T
+            return carry
+
+        lax.fori_loop(0, 4, step, 0)
+
+    turned = [copy(ata.at[here], ata.at[here], k_s.at[0], k_r.at[0], partner),
+              copy(atb.at[c], atb.at[c], k_s.at[1], k_r.at[1], partner)]
+    turn_a(0)
     swap.wait_recv()
     sm[...] = part_gram[own_half] + d2[...]
     up, down, across = mod4(x + 1), mod4(x + 3), mod4(x + 2)
@@ -265,20 +266,18 @@
              copy(sm.at[rows_of(down)], x3.at[1], m_s.at[3], m_r.at[3], dev_down)]
     share[0].start()
     share[1].start()
-    for r in range(4):
-        block = ao.at[mod4(x + 4 - r), there]
-        copy(block, block, k_s.at[r], k_r.at[r], partner).wait_recv()
     r_by[0].forward()
     r_by[3].start()
     r_by[1].start()
-    turn(0)
+    turn_a(1)
+    turned[0].start()
     share[0].wait_recv()
     sm[pl.ds(pl.multiple_of(up * SEG, 8), 48)] += near_a[...]
     share[2].start()
     share[1].wait_recv()
     sm[pl.ds(pl.multiple_of(down * SEG + 48, 8), 40)] += near_b[...]
     share[3].start()
-    turn(1)
+    turn_b(0)
 
     r_cg.finish()
     r_ay.finish()
@@ -290,12 +289,14 @@
     full[rows_of(4 * c + x)] = sm[rows_of(x)] + x3[0] + x3[1]
     r_full.start()
     r_az[0].forward()
-    turn(2)
+    turn_b(1)
     r_full.forward()
-    turn(3)
+    turn_b(2)
     r_full.finish()
     give = copy(full.at[own_half], full.at[own_half], d_s.at[1], d_r.at[1], partner)
     give.start()
+    turn_b(3)
+    turned[1].start()
 
     r_bz.finish()
     r_by[2].start()
@@ -335,22 +336,27 @@
     tile = sum_tiles(sv2, 4 * z + y, 16, 8)
     weights = jnp.maximum(-tile, 0.0) / jnp.sum(jnp.abs(tile), axis=0, keepdims=True)
     wts[...] = weights
-    for k in range(4):
-        scale[k, :SEG] = jnp.broadcast_to(wts[2 * k:2 * k + 1, :], (SEG, LANES))
-        scale[k, SEG:] = jnp.broadcast_to(wts[2 * k + 1:2 * k + 2, :], (SEG, LANES))
     lane = lax.broadcasted_iota(jnp.int32, (1, LANES), 1)
     wout_ref[...] = jnp.where(lane == 0, wts[pl.ds(2 * z, 1), :], wts[pl.ds(2 * z + 1, 1), :])[:, :2]
 
-    def scaled(raw, s):
-        full = jnp.concatenate([s] * (raw.shape[1] // LANES), axis=1)
-        return (raw.astype(F32) * full).astype(BF16)
-
-    def product(at, pieces_of, width, base, first, span):
+    copy(ata.at[there], ata.at[there], k_s.at[0], k_r.at[0], partner).wait_recv()
+    copy(atb.at[1 - c], atb.at[1 - c], k_s.at[1], k_r.at[1], partner).wait_recv()
+
+    def scaled(rows_in, k):
+        width = rows_in.shape[1]
+
+        def part(j):
+            row = wts[pl.ds(2 * k + j, 1), :]
+            factor = jnp.broadcast_to(jnp.concatenate([row] * (width // LANES), axis=1), (SEG, width))
+            return rows_in[j * SEG:(j + 1) * SEG] * factor
+
+        return jnp.concatenate([part(0), part(1)], axis=0).astype(BF16)
+
+    def product(left_of, right_of, width, base, first, span):
         def step(i, carry):
             cols = pl.ds(pl.multiple_of(i * span, span), span)
             dest = pl.ds(pl.multiple_of(base + i * span, 256), span)
-            right = jnp.concatenate([scaled(raw, s) for raw, s in pieces_of(cols)], axis=0)
-            value = jnp.dot(at[...], right, preferred_element_type=F32)
+            value = jnp.dot(left_of(), right_of(cols), preferred_element_type=F32)
             if first:
                 out_ref[:, dest] = value
             else:
@@ -361,11 +367,21 @@
 
     def add_a(k, first=False):
         v = mod4(z + k)
-        product(ata.at[v], lambda cols: [(ga[v, i, :, cols], scale[v]) for i in range(4)], WA, 0, first, 768)
+
+        def right_of(cols):
+            return jnp.concatenate([scaled(ga[v, i, :, cols].astype(F32), v) for i in range(4)], axis=0)
+
+        product(lambda: ata[v], right_of, WA, 0, first, 768)
 
     def add_b(k, first=False):
         v = mod4(y + k)
-        product(atb.at[v], lambda cols: [(gb[v, i, :, cols], scale[i]) for i in range(4)], WB, WA, first, 512)
+
+        def right_of(cols):
+            parts = [scaled(gb[v, i, :, cols].astype(F32), i) for i in range(4)]
+            empty = jnp.zeros((32, 512), BF16)
+            return jnp.concatenate([parts[0], parts[1], empty, parts[2], parts[3], empty], axis=0)
+
+        product(lambda: jnp.concatenate([atb[0, v], atb[1, v]], axis=1), right_of, WB, WA, first, 512)
 
     add_a(0, True)
     r_az[1].forward()
@@ -390,7 +406,7 @@
             far_copy.wait_send()
     for ring in rings:
         ring.drain()
-    for k in core + [swap, give] + share + sends:
+    for k in turned + [swap, give] + share + sends:
         k.wait_send()
 
 
@@ -410,7 +426,7 @@
             vmem((4, 4, NOISE, WB), BF16),
             vmem((4, 4, 4, NOISE, LANES), BF16),
             vmem((4, 512, 4 * NOISE), BF16),
-            vmem((4, 512, 4 * NOISE), BF16),
+            vmem((2, 4, 512, 384), BF16),
             vmem((4 * NOISE, 4 * CLEAN_ROWS), F32),
             vmem((4 * NOISE, 4 * CLEAN_ROWS), F32),
             vmem((4 * NOISE, 4 * CLEAN_ROWS), F32),
@@ -422,10 +438,9 @@
             vmem((8, 8, LANES), F32),
             vmem((16, 8, LANES), F32),
             vmem((8, LANES), F32),
-            vmem((4, NOISE, LANES), F32),
             dma((15, 4)), dma((15, 4)),
             dma((8,)), dma((8,)), dma,
-            dma((4,)), dma((4,)),
+            dma((2,)), dma((2,)),
             dma((2,)), dma((2,)),
             dma((4,)), dma((4,)),
             dma((24,)), dma((24,)),

time: 91.3 us -> 91.2 us (level)
  no operation moved by 1% of the time
where the time goes in v5:
time: 91.2 us; the launch traced here: 91.1 us
  Pallas kernels  88.1 us (97%)
  local copies, waits for them, and re-layouts  2.35 us (3%)
    pallas_call x1, Pallas kernels, body(): pl.pallas_call(body_kernel, out_shape=(pltpu.VMEM((512, WA + WB), F32), p...  88.1 us
    unnamed x2, local copies, waits for them, and re-layouts  2.35 us

profile of v5, /device:TPU:0, one launch (start us, length us, event | category | flops | bytes accessed | tf_op | source)
XLA Modules:
  0.0 91.1 jit_solution(9935168857541001754)
XLA Ops:
  0.6 88.1 %reweight.1 = (f32[512,1792]{1,0:T(8,128)S(1)}, f32[1,2]{1,0:T(1,128)S(1)}) custom-call(s32[1,3]{1,0:T(1,128)} %ids_ref.1, s32[1,3]{1,0:T(1,128)} %counts_ref.1, bf16[3,88,1024]{2,1,0:T(8,128)(2,1)} %acts_ref.1, bf16[3,88,1792]{2,1,0:T(8,128)(2,1)} %cot_ref.1), custom_call_target="tpu_custom_call" | custom-call | flops 8000000000 | bytes 8000000 | tf_op jit(solution)/shard_map/reweight/pallas_call | solution.py:416
  88.7 1.8 %copy.8 = f32[512,1792]{1,0:T(8,128)} copy(f32[512,1792]{1,0:T(8,128)S(1)} %get-tuple-element.2) | data formatting | bytes 7340032
  90.6 0.5 copy.9

commit v6 on v5

--- a/solution.py
+++ b/solution.py
@@ -195,24 +195,10 @@
     r_bz.start()
     r_na.forward()
     r_by[0].start()
-    for i, ((zs, ys), same) in enumerate(zip(sources, source_self)):
-        dst = ao.at[x, zs, ys]
-        far_copy = copy(dst, dst, p_s.at[i], p_r.at[i], (z, y, lax.rem(t + 1, 8)))
-        near_copy = pltpu.make_async_copy(dst, dst, p_l)
-
-        @pl.when(same)
-        def _():
-            near_copy.wait()
-
-        @pl.when(jnp.logical_not(same))
-        def _():
-            far_copy.wait_recv()
     partner = (z, y, 2 * x + 1 - c)
-    r_ao.start()
     r_cg.forward()
     r_az[0].start()
     r_ay.forward()
-    r_ao.forward()
 
     contract = (((1,), (1,)), ((), ()))
 
@@ -227,10 +213,22 @@
     swap = copy(part_gram.at[other_half], d2, d_s.at[0], d_r.at[0], partner)
     swap.start()
 
-    r_ao.finish()
     r_bz.forward()
     r_az[3].start()
     r_az[1].start()
+    for i, ((zs, ys), same) in enumerate(zip(sources, source_self)):
+        dst = ao.at[x, zs, ys]
+        far_copy = copy(dst, dst, p_s.at[i], p_r.at[i], (z, y, lax.rem(t + 1, 8)))
+        near_copy = pltpu.make_async_copy(dst, dst, p_l)
+
+        @pl.when(same)
+        def _():
+            near_copy.wait()
+
+        @pl.when(jnp.logical_not(same))
+        def _():
+            far_copy.wait_recv()
+    r_ao.start()
 
     def turn_a(k):
         def step(q, carry):
@@ -253,7 +251,6 @@
 
     turned = [copy(ata.at[here], ata.at[here], k_s.at[0], k_r.at[0], partner),
               copy(atb.at[c], atb.at[c], k_s.at[1], k_r.at[1], partner)]
-    turn_a(0)
     swap.wait_recv()
     sm[...] = part_gram[own_half] + d2[...]
     up, down, across = mod4(x + 1), mod4(x + 3), mod4(x + 2)
@@ -269,15 +266,13 @@
     r_by[0].forward()
     r_by[3].start()
     r_by[1].start()
-    turn_a(1)
-    turned[0].start()
     share[0].wait_recv()
     sm[pl.ds(pl.multiple_of(up * SEG, 8), 48)] += near_a[...]
     share[2].start()
     share[1].wait_recv()
     sm[pl.ds(pl.multiple_of(down * SEG + 48, 8), 40)] += near_b[...]
     share[3].start()
-    turn_b(0)
+    r_ao.forward()
 
     r_cg.finish()
     r_ay.finish()
@@ -289,14 +284,14 @@
     full[rows_of(4 * c + x)] = sm[rows_of(x)] + x3[0] + x3[1]
     r_full.start()
     r_az[0].forward()
-    turn_b(1)
     r_full.forward()
-    turn_b(2)
+    r_ao.finish()
+    turn_a(0)
     r_full.finish()
     give = copy(full.at[own_half], full.at[own_half], d_s.at[1], d_r.at[1], partner)
     give.start()
-    turn_b(3)
-    turned[1].start()
+    turn_a(1)
+    turned[0].start()
 
     r_bz.finish()
     r_by[2].start()
@@ -329,6 +324,9 @@
 
     send_tile(sv1, tile, t, 8, lambda r: (z, y, lax.rem(t + r, 8)), 0)
 
+    for v in range(4):
+        turn_b(v)
+    turned[1].start()
     tile = sum_tiles(sv1, t, 8, 0)
     send_tile(sv2, tile, 4 * z + y, 16, cell, 8)
     r_az[3].forward()

time: 91.2 us -> 92.6 us (1.015)
  Pallas kernels: 88.1 us -> 89.5 us
    pallas_call x1, Pallas kernels: 88.1 us -> 89.5 us  [body(): pl.pallas_call(body_kernel, out_shape=(pltpu.VMEM((512, WA + WB), F32), p...]
where the time goes in v6:
time: 92.6 us; the launch traced here: 92.5 us
  Pallas kernels  89.5 us (97%)
  local copies, waits for them, and re-layouts  2.35 us (3%)
    pallas_call x1, Pallas kernels, body(): pl.pallas_call(body_kernel, out_shape=(pltpu.VMEM((512, WA + WB), F32), p...  89.5 us
    unnamed x2, local copies, waits for them, and re-layouts  2.35 us

profile of v6, /device:TPU:0, one launch (start us, length us, event | category | flops | bytes accessed | tf_op | source)
XLA Modules:
  0.0 92.5 jit_solution(11408674868994711406)
XLA Ops:
  0.6 89.5 %reweight.1 = (f32[512,1792]{1,0:T(8,128)S(1)}, f32[1,2]{1,0:T(1,128)S(1)}) custom-call(s32[1,3]{1,0:T(1,128)} %ids_ref.1, s32[1,3]{1,0:T(1,128)} %counts_ref.1, bf16[3,88,1024]{2,1,0:T(8,128)(2,1)} %acts_ref.1, bf16[3,88,1792]{2,1,0:T(8,128)(2,1)} %cot_ref.1), custom_call_target="tpu_custom_call" | custom-call | flops 8000000000 | bytes 8000000 | tf_op jit(solution)/shard_map/reweight/pallas_call | solution.py:414
  90.1 1.8 %copy.8 = f32[512,1792]{1,0:T(8,128)} copy(f32[512,1792]{1,0:T(8,128)S(1)} %get-tuple-element.2) | data formatting | bytes 7340032
  92.0 0.5 copy.9

commit v7 on v6

--- a/solution.py
+++ b/solution.py
@@ -18,9 +18,9 @@
 
 
 def body_kernel(ids_ref, counts_ref, acts_ref, cot_ref, out_ref, wout_ref,
-                na, ca, cg, ga, gb, ao, ata, atb, part_gram, grad_gram, full, d2, sm,
+                na, ca, cg, ga, gb, hop, ao, ata, atb, part_gram, grad_gram, full, d2, sm,
                 near_a, near_b, x3, sv1, sv2, wts,
-                ring_s, ring_r, p_s, p_r, p_l, k_s, k_r,
+                ring_s, ring_r, h_s, h_r, p_s, p_r, p_l, k_s, k_r,
                 d_s, d_r, m_s, m_r, v_s, v_r):
     z = lax.axis_index("dp")
     y = lax.axis_index("seq")
@@ -49,10 +49,10 @@
     for r in range(1, 8):
         greet((z, y, lax.rem(t + r, 8)))
 
-    targets = [(h, q, (x, 2 * c + h, 2 * q + z // 2)) for h in range(2) for q in range(4)]
-    target_self = [(x == z) & (y == 2 * c + h) & (q == x) & (c == z // 2) for h, q, _ in targets]
+    targets = [(r, h, (mod4(x + r), 2 * c + h, 2 * x + z // 2)) for r in range(4) for h in range(2)]
+    target_self = [(dev[0] == z) & (dev[1] == y) & (c == z // 2) for _, _, dev in targets]
     sources = [(2 * c + i // 4, i % 4) for i in range(8)]
-    source_self = [(zs == z) & (ys == y) & (x == z) & (c == y // 2) for zs, ys in sources]
+    source_self = [(zs == z) & (ys == y) & (c == y // 2) for zs, ys in sources]
     for (_, _, dev), same in zip(targets, target_self):
         @pl.when(jnp.logical_not(same))
         def _():
@@ -60,8 +60,8 @@
     for (zs, ys), same in zip(sources, source_self):
         @pl.when(jnp.logical_not(same))
         def _():
-            greet((zs, ys, 2 * z + y // 2))
-    has_self = ((x == z) & (c == y // 2) & (c == z // 2)).astype(jnp.int32)
+            greet((zs, ys, 2 * x + y // 2))
+    has_self = ((c == y // 2) & (c == z // 2)).astype(jnp.int32)
 
     rid = [ids_ref[0, j] for j in range(3)]
     live = [counts_ref[0, rid[j]] - y * SEG for j in range(3)]
@@ -99,10 +99,26 @@
 
     pl.semaphore_wait(barrier, 38 - 2 * has_self)
 
+    hops = []
+    for r in range(1, 4):
+        q = mod4(x + r)
+        for h in range(2):
+            src = na.at[y, :, pl.ds(pl.multiple_of(h * 512 + q * LANES, LANES), LANES)]
+            hops.append(copy(src, hop.at[r, h], h_s.at[r, h], h_r.at[r, h], (z, y, 2 * q + c)))
+    for k in hops:
+        k.start()
+
     pieces = []
-    for i, ((h, q, dev), same) in enumerate(zip(targets, target_self)):
-        src = na.at[y, :, pl.ds(h * 512 + q * LANES, LANES)]
-        dst = ao.at[q, z, y]
+
+    def send_piece(i):
+        r, h, dev = targets[i]
+        same = target_self[i]
+        if r:
+            src = hop.at[4 - r, h]
+            copy(src, src, h_s.at[4 - r, h], h_r.at[4 - r, h], (z, y, lax.rem(t + 1, 8))).wait_recv()
+        else:
+            src = na.at[y, :, pl.ds(pl.multiple_of(h * 512 + x * LANES, LANES), LANES)]
+        dst = ao.at[x, z, y]
         far_copy = copy(src, dst, p_s.at[i], p_r.at[lax.rem(z, 2) * 4 + y], dev)
         near_copy = pltpu.make_async_copy(src, dst, p_l)
 
@@ -113,7 +129,7 @@
         @pl.when(jnp.logical_not(same))
         def _():
             far_copy.start()
-        pieces.append((far_copy, near_copy, same))
+        pieces.append((far_copy, same))
 
     rings = []
 
@@ -186,10 +202,12 @@
     r_na.start()
     r_ca.start()
     lax.fori_loop(0, WA // LANES, stage_a, 0)
+    lax.fori_loop(0, (WA + WB) // LANES, stage_clean, 0)
+    lax.fori_loop(0, WB // LANES, stage_b, 0)
+    for i in range(8):
+        send_piece(i)
     r_ay.start()
-    lax.fori_loop(0, (WA + WB) // LANES, stage_clean, 0)
     r_cg.start()
-    lax.fori_loop(0, WB // LANES, stage_b, 0)
 
     r_ca.forward()
     r_bz.start()
@@ -398,13 +416,13 @@
         r_by[k].finish()
     add_b(2)
 
-    for far_copy, _, same in pieces:
+    for far_copy, same in pieces:
         @pl.when(jnp.logical_not(same))
         def _():
             far_copy.wait_send()
     for ring in rings:
         ring.drain()
-    for k in turned + [swap, give] + share + sends:
+    for k in hops + turned + [swap, give] + share + sends:
         k.wait_send()
 
 
@@ -422,6 +440,7 @@
             vmem((4, CLEAN_ROWS, WA + WB), BF16),
             vmem((4, 4, NOISE, WA), BF16),
             vmem((4, 4, NOISE, WB), BF16),
+            vmem((4, 2, NOISE, LANES), BF16),
             vmem((4, 4, 4, NOISE, LANES), BF16),
             vmem((4, 512, 4 * NOISE), BF16),
             vmem((2, 4, 512, 384), BF16),
@@ -437,6 +456,7 @@
             vmem((16, 8, LANES), F32),
             vmem((8, LANES), F32),
             dma((15, 4)), dma((15, 4)),
+            dma((4, 2)), dma((4, 2)),
             dma((8,)), dma((8,)), dma,
             dma((2,)), dma((2,)),
             dma((2,)), dma((2,)),

time: 92.6 us -> 94.1 us (1.016)
  Pallas kernels: 89.5 us -> 90.9 us
    pallas_call x1, Pallas kernels: 89.5 us -> 90.9 us  [body(): pl.pallas_call(body_kernel, out_shape=(pltpu.VMEM((512, WA + WB), F32), p...]
where the time goes in v7:
time: 94.1 us; the launch traced here: 93.9 us
  Pallas kernels  90.9 us (97%)
  local copies, waits for them, and re-layouts  2.35 us (2%)
    pallas_call x1, Pallas kernels, body(): pl.pallas_call(body_kernel, out_shape=(pltpu.VMEM((512, WA + WB), F32), p...  90.9 us
    unnamed x2, local copies, waits for them, and re-layouts  2.35 us

profile of v7, /device:TPU:0, one launch (start us, length us, event | category | flops | bytes accessed | tf_op | source)
XLA Modules:
  0.0 93.9 jit_solution(12990252993338921600)
XLA Ops:
  0.6 90.9 %reweight.1 = (f32[512,1792]{1,0:T(8,128)S(1)}, f32[1,2]{1,0:T(1,128)S(1)}) custom-call(s32[1,3]{1,0:T(1,128)} %ids_ref.1, s32[1,3]{1,0:T(1,128)} %counts_ref.1, bf16[3,88,1024]{2,1,0:T(8,128)(2,1)} %acts_ref.1, bf16[3,88,1792]{2,1,0:T(8,128)(2,1)} %cot_ref.1), custom_call_target="tpu_custom_call" | custom-call | flops 8000000000 | bytes 8000000 | tf_op jit(solution)/shard_map/reweight/pallas_call | solution.py:432
  91.6 1.8 %copy.8 = f32[512,1792]{1,0:T(8,128)} copy(f32[512,1792]{1,0:T(8,128)S(1)} %get-tuple-element.2) | data formatting | bytes 7340032
  93.4 0.5 copy.9

commit v8 on v5

--- a/solution.py
+++ b/solution.py
@@ -162,16 +162,16 @@
 
     def az_ring(k):
         item = mod4(y + k)
-        return Ring(lambda v: ga.at[v, item], "z", *(even if k in (0, 1) else odd))
+        return Ring(lambda v: ga.at[v, item], "z", *odd)
 
     def by_ring(k):
         item = mod4(z + k)
-        return Ring(lambda v: gb.at[v, item], "y", *(even if k in (0, 1) else odd))
+        return Ring(lambda v: gb.at[v, item], "y", *odd)
 
     def rows_of(chunk):
         return pl.ds(pl.multiple_of(chunk * SEG, 8), SEG)
 
-    r_na = Ring(lambda v: na.at[v], "y", *even)
+    r_na = Ring(lambda v: na.at[v], "y", *odd)
     r_ca = Ring(lambda v: ca.at[v], "z", *equal)
     r_cg = Ring(lambda v: cg.at[v], "z", *equal)
     r_ay = Ring(lambda v: ga.at[z, v], "y", *odd)

time: 91.2 us -> 91.2 us (level)
  no operation moved by 1% of the time
where the time goes in v8:
time: 91.2 us; the launch traced here: 91.1 us
  Pallas kernels  88.1 us (97%)
  local copies, waits for them, and re-layouts  2.35 us (3%)
    pallas_call x1, Pallas kernels, body(): pl.pallas_call(body_kernel, out_shape=(pltpu.VMEM((512, WA + WB), F32), p...  88.1 us
    unnamed x2, local copies, waits for them, and re-layouts  2.35 us

profile of v8, /device:TPU:0, one launch (start us, length us, event | category | flops | bytes accessed | tf_op | source)
XLA Modules:
  0.0 91.1 jit_solution(2026129918229504581)
XLA Ops:
  0.6 88.1 %reweight.1 = (f32[512,1792]{1,0:T(8,128)S(1)}, f32[1,2]{1,0:T(1,128)S(1)}) custom-call(s32[1,3]{1,0:T(1,128)} %ids_ref.1, s32[1,3]{1,0:T(1,128)} %counts_ref.1, bf16[3,88,1024]{2,1,0:T(8,128)(2,1)} %acts_ref.1, bf16[3,88,1792]{2,1,0:T(8,128)(2,1)} %cot_ref.1), custom_call_target="tpu_custom_call" | custom-call | flops 8000000000 | bytes 8000000 | tf_op jit(solution)/shard_map/reweight/pallas_call | solution.py:416
  88.7 1.8 %copy.8 = f32[512,1792]{1,0:T(8,128)} copy(f32[512,1792]{1,0:T(8,128)S(1)} %get-tuple-element.2) | data formatting | bytes 7340032
  90.6 0.5 copy.9

commit v9 on v8

--- a/solution.py
+++ b/solution.py
@@ -156,26 +156,25 @@
             for k in self.go + self.pass_on:
                 k.wait_send()
 
-    even = (pl.ds(0, 96),), (pl.ds(96, 80),)
-    odd = (pl.ds(80, 96),), (pl.ds(0, 80),)
+    uneven = (pl.ds(0, 80),), (pl.ds(80, 96),)
     equal = (pl.ds(0, 48),), (pl.ds(48, 48),)
 
     def az_ring(k):
         item = mod4(y + k)
-        return Ring(lambda v: ga.at[v, item], "z", *odd)
+        return Ring(lambda v: ga.at[v, item], "z", *uneven)
 
     def by_ring(k):
         item = mod4(z + k)
-        return Ring(lambda v: gb.at[v, item], "y", *odd)
+        return Ring(lambda v: gb.at[v, item], "y", *uneven)
 
     def rows_of(chunk):
         return pl.ds(pl.multiple_of(chunk * SEG, 8), SEG)
 
-    r_na = Ring(lambda v: na.at[v], "y", *odd)
+    r_na = Ring(lambda v: na.at[v], "y", *uneven)
     r_ca = Ring(lambda v: ca.at[v], "z", *equal)
     r_cg = Ring(lambda v: cg.at[v], "z", *equal)
-    r_ay = Ring(lambda v: ga.at[z, v], "y", *odd)
-    r_bz = Ring(lambda v: gb.at[y, v], "z", *odd)
+    r_ay = Ring(lambda v: ga.at[z, v], "y", *uneven)
+    r_bz = Ring(lambda v: gb.at[y, v], "z", *uneven)
     r_az = {k: az_ring(k) for k in (0, 3, 1, 2)}
     r_by = {k: by_ring(k) for k in (0, 3, 1, 2)}
     here = pl.ds(2 * c, 2)

time: 91.2 us -> 92.2 us (1.011); the launches traced: 91.1 us -> 91.1 us
  no operation moved by 1% of the time
where the time goes in v9:
time: 92.2 us; the launch traced here: 91.1 us
  Pallas kernels  88.1 us (96%)
  local copies, waits for them, and re-layouts  2.35 us (3%)
    pallas_call x1, Pallas kernels, body(): pl.pallas_call(body_kernel, out_shape=(pltpu.VMEM((512, WA + WB), F32), p...  88.1 us
    unnamed x2, local copies, waits for them, and re-layouts  2.35 us

profile of v9, /device:TPU:0, one launch (start us, length us, event | category | flops | bytes accessed | tf_op | source)
XLA Modules:
  0.0 91.1 jit_solution(6245872313506280538)
XLA Ops:
  0.6 88.1 %reweight.1 = (f32[512,1792]{1,0:T(8,128)S(1)}, f32[1,2]{1,0:T(1,128)S(1)}) custom-call(s32[1,3]{1,0:T(1,128)} %ids_ref.1, s32[1,3]{1,0:T(1,128)} %counts_ref.1, bf16[3,88,1024]{2,1,0:T(8,128)(2,1)} %acts_ref.1, bf16[3,88,1792]{2,1,0:T(8,128)(2,1)} %cot_ref.1), custom_call_target="tpu_custom_call" | custom-call | flops 8000000000 | bytes 8000000 | tf_op jit(solution)/shard_map/reweight/pallas_call | solution.py:415
  88.7 1.8 %copy.8 = f32[512,1792]{1,0:T(8,128)} copy(f32[512,1792]{1,0:T(8,128)S(1)} %get-tuple-element.2) | data formatting | bytes 7340032
  90.6 0.5 copy.9

commit v10 on v5

--- a/solution.py
+++ b/solution.py
@@ -185,15 +185,14 @@
 
     r_na.start()
     r_ca.start()
-    lax.fori_loop(0, WA // LANES, stage_a, 0)
-    r_ay.start()
     lax.fori_loop(0, (WA + WB) // LANES, stage_clean, 0)
     r_cg.start()
+    lax.fori_loop(0, WA // LANES, stage_a, 0)
     lax.fori_loop(0, WB // LANES, stage_b, 0)
 
     r_ca.forward()
-    r_bz.start()
     r_na.forward()
+    r_ay.start()
     r_by[0].start()
     for i, ((zs, ys), same) in enumerate(zip(sources, source_self)):
         dst = ao.at[x, zs, ys]
@@ -210,9 +209,8 @@
     partner = (z, y, 2 * x + 1 - c)
     r_ao.start()
     r_cg.forward()
+    r_bz.start()
     r_az[0].start()
-    r_ay.forward()
-    r_ao.forward()
 
     contract = (((1,), (1,)), ((), ()))
 
@@ -226,11 +224,8 @@
     other_half = pl.ds(pl.multiple_of((1 - c) * 352, 8), 352)
     swap = copy(part_gram.at[other_half], d2, d_s.at[0], d_r.at[0], partner)
     swap.start()
-
-    r_ao.finish()
-    r_bz.forward()
-    r_az[3].start()
-    r_az[1].start()
+    r_ay.forward()
+
 
     def turn_a(k):
         def step(q, carry):
@@ -253,7 +248,6 @@
 
     turned = [copy(ata.at[here], ata.at[here], k_s.at[0], k_r.at[0], partner),
               copy(atb.at[c], atb.at[c], k_s.at[1], k_r.at[1], partner)]
-    turn_a(0)
     swap.wait_recv()
     sm[...] = part_gram[own_half] + d2[...]
     up, down, across = mod4(x + 1), mod4(x + 3), mod4(x + 2)
@@ -266,40 +260,34 @@
              copy(sm.at[rows_of(down)], x3.at[1], m_s.at[3], m_r.at[3], dev_down)]
     share[0].start()
     share[1].start()
-    r_by[0].forward()
-    r_by[3].start()
-    r_by[1].start()
-    turn_a(1)
-    turned[0].start()
+    r_ao.forward()
     share[0].wait_recv()
     sm[pl.ds(pl.multiple_of(up * SEG, 8), 48)] += near_a[...]
     share[2].start()
     share[1].wait_recv()
     sm[pl.ds(pl.multiple_of(down * SEG + 48, 8), 40)] += near_b[...]
     share[3].start()
-    turn_b(0)
-
-    r_cg.finish()
-    r_ay.finish()
-    r_az[2].start()
-    grad_gram[...] = gram(ga[z].reshape(4 * NOISE, WA), cg[:, :, :WA].reshape(4 * CLEAN_ROWS, WA))
+    r_bz.forward()
 
     share[2].wait_recv()
     share[3].wait_recv()
     full[rows_of(4 * c + x)] = sm[rows_of(x)] + x3[0] + x3[1]
     r_full.start()
-    r_az[0].forward()
-    turn_b(1)
+    r_by[0].forward()
+    r_by[3].start()
+    r_az[3].start()
     r_full.forward()
-    turn_b(2)
     r_full.finish()
     give = copy(full.at[own_half], full.at[own_half], d_s.at[1], d_r.at[1], partner)
     give.start()
-    turn_b(3)
-    turned[1].start()
-
-    r_bz.finish()
-    r_by[2].start()
+    r_cg.finish()
+    r_ay.finish()
+    grad_gram[...] = gram(ga[z].reshape(4 * NOISE, WA), cg[:, :, :WA].reshape(4 * CLEAN_ROWS, WA))
+    r_ao.finish()
+    turn_a(0)
+    turn_a(1)
+    turned[0].start()
+
     r_by[0].finish()
     grad_gram[...] += gram(gb[:, z].reshape(4 * NOISE, WB), cg[:, :, WA:].reshape(4 * CLEAN_ROWS, WB))
     copy(full.at[other_half], full.at[other_half], d_s.at[1], d_r.at[1], partner).wait_recv()
@@ -329,8 +317,17 @@
 
     send_tile(sv1, tile, t, 8, lambda r: (z, y, lax.rem(t + r, 8)), 0)
 
+    r_az[0].forward()
     tile = sum_tiles(sv1, t, 8, 0)
     send_tile(sv2, tile, 4 * z + y, 16, cell, 8)
+    r_by[1].start()
+    r_az[1].start()
+    r_az[2].start()
+    r_bz.finish()
+    r_by[2].start()
+    for v in range(4):
+        turn_b(v)
+    turned[1].start()
     r_az[3].forward()
     r_by[3].forward()
     tile = sum_tiles(sv2, 4 * z + y, 16, 8)

time: 91.2 us -> 98.8 us (1.083)
  Pallas kernels: 88.1 us -> 95.1 us
    pallas_call x1, Pallas kernels: 88.1 us -> 95.1 us  [body(): pl.pallas_call(body_kernel, out_shape=(pltpu.VMEM((512, WA + WB), F32), p...]
where the time goes in v10:
time: 98.8 us; the launch traced here: 98.1 us
  Pallas kernels  95.1 us (96%)
  local copies, waits for them, and re-layouts  2.35 us (2%)
    pallas_call x1, Pallas kernels, body(): pl.pallas_call(body_kernel, out_shape=(pltpu.VMEM((512, WA + WB), F32), p...  95.1 us
    unnamed x2, local copies, waits for them, and re-layouts  2.35 us

profile of v10, /device:TPU:0, one launch (start us, length us, event | category | flops | bytes accessed | tf_op | source)
XLA Modules:
  0.0 98.1 jit_solution(8480200718479567322)
XLA Ops:
  0.6 95.1 %reweight.1 = (f32[512,1792]{1,0:T(8,128)S(1)}, f32[1,2]{1,0:T(1,128)S(1)}) custom-call(s32[1,3]{1,0:T(1,128)} %ids_ref.1, s32[1,3]{1,0:T(1,128)} %counts_ref.1, bf16[3,88,1024]{2,1,0:T(8,128)(2,1)} %acts_ref.1, bf16[3,88,1792]{2,1,0:T(8,128)(2,1)} %cot_ref.1), custom_call_target="tpu_custom_call" | custom-call | flops 8000000000 | bytes 8000000 | tf_op jit(solution)/shard_map/reweight/pallas_call | solution.py:413
  95.8 1.8 %copy.8 = f32[512,1792]{1,0:T(8,128)} copy(f32[512,1792]{1,0:T(8,128)S(1)} %get-tuple-element.2) | data formatting | bytes 7340032
  97.6 0.5 copy.9

commit v11 on v10

--- a/solution.py
+++ b/solution.py
@@ -11,14 +11,15 @@
 
 SEG = 88
 NOISE = 176
-CLEAN_ROWS = 96
+CLEAN_ROWS = 88
+HALF = 896
 WA = 768
 WB = 1024
 LANES = 128
 
 
 def body_kernel(ids_ref, counts_ref, acts_ref, cot_ref, out_ref, wout_ref,
-                na, ca, cg, ga, gb, ao, ata, atb, part_gram, grad_gram, full, d2, sm,
+                na, ca, cg, left, right, ga, gb, ao, ata, atb, part_gram, grad_gram, full, d2, sm,
                 near_a, near_b, x3, sv1, sv2, wts,
                 ring_s, ring_r, p_s, p_r, p_l, k_s, k_r,
                 d_s, d_r, m_s, m_r, v_s, v_r):
@@ -49,40 +50,49 @@
     for r in range(1, 8):
         greet((z, y, lax.rem(t + r, 8)))
 
-    targets = [(h, q, (x, 2 * c + h, 2 * q + z // 2)) for h in range(2) for q in range(4)]
-    target_self = [(x == z) & (y == 2 * c + h) & (q == x) & (c == z // 2) for h, q, _ in targets]
+    active = c == y // 2
+    targets = [(x, y, 2 * q + z // 2) for q in range(4)]
+    target_self = [active & (x == z) & (q == x) & (c == z // 2) for q in range(4)]
     sources = [(2 * c + i // 4, i % 4) for i in range(8)]
-    source_self = [(zs == z) & (ys == y) & (x == z) & (c == y // 2) for zs, ys in sources]
-    for (_, _, dev), same in zip(targets, target_self):
-        @pl.when(jnp.logical_not(same))
+    source_self = [(zs == z) & (x == z) & active for zs, _ in sources]
+    for dev, same in zip(targets, target_self):
+        @pl.when(active & jnp.logical_not(same))
         def _():
             greet(dev)
-    for (zs, ys), same in zip(sources, source_self):
-        @pl.when(jnp.logical_not(same))
+    for i in (0, 4):
+        @pl.when(jnp.logical_not(source_self[i]))
         def _():
-            greet((zs, ys, 2 * z + y // 2))
-    has_self = ((x == z) & (c == y // 2) & (c == z // 2)).astype(jnp.int32)
+            greet((sources[i][0], y, 2 * z + y // 2))
+    sends_here = active.astype(jnp.int32)
+    has_self = (active & (x == z) & (c == z // 2)).astype(jnp.int32)
 
     rid = [ids_ref[0, j] for j in range(3)]
     live = [counts_ref[0, rid[j]] - y * SEG for j in range(3)]
     rows = lax.broadcasted_iota(jnp.int32, (SEG, LANES), 0)
-    pad = jnp.zeros((CLEAN_ROWS - SEG, LANES), F32)
+
+    def block_of(i, base=0):
+        return pl.ds(pl.multiple_of(base + i * LANES, LANES), LANES)
 
     def stage_acts(i, carry):
-        cols = pl.ds(pl.multiple_of(i * LANES, LANES), LANES)
-        part = [acts_ref[rid[j], :, cols].astype(F32) for j in range(3)]
-        na[y, :, cols] = jnp.concatenate([part[1], part[2]], axis=0).astype(BF16)
-        ca[z, :, cols] = jnp.concatenate([part[0], pad], axis=0).astype(BF16)
+        cols = block_of(i)
+        part = [acts_ref[rid[j], :, cols].astype(F32) for j in (1, 2)]
+        na[y, :, cols] = jnp.concatenate(part, axis=0).astype(BF16)
         return carry
 
+    def stage_clean_acts(i, carry):
+        part = [acts_ref[rid[0], :, block_of(i, base)].astype(F32) for base in (0, 512)]
+        ca[z, :, block_of(i)] = jnp.concatenate(part, axis=0).astype(BF16)
+        return carry
+
     lax.fori_loop(0, 1024 // LANES, stage_acts, 0)
+    lax.fori_loop(0, 512 // LANES, stage_clean_acts, 0)
 
     def masked(j, cols):
         return jnp.where(rows < live[j], cot_ref[rid[j], :, cols].astype(F32), 0.0)
 
     def stage_clean(i, carry):
-        cols = pl.ds(pl.multiple_of(i * LANES, LANES), LANES)
-        cg[z, :, cols] = jnp.concatenate([masked(0, cols), pad], axis=0).astype(BF16)
+        part = [masked(0, block_of(i, base)) for base in (0, HALF)]
+        cg[z, :, block_of(i)] = jnp.concatenate(part, axis=0).astype(BF16)
         return carry
 
     def stage_a(i, carry):
@@ -97,23 +107,43 @@
             [masked(1, from_cols), masked(2, from_cols)], axis=0).astype(BF16)
         return carry
 
-    pl.semaphore_wait(barrier, 38 - 2 * has_self)
+    pl.semaphore_wait(barrier, 24 + 4 * sends_here - 2 * has_self)
 
     pieces = []
-    for i, ((h, q, dev), same) in enumerate(zip(targets, target_self)):
-        src = na.at[y, :, pl.ds(h * 512 + q * LANES, LANES)]
-        dst = ao.at[q, z, y]
-        far_copy = copy(src, dst, p_s.at[i], p_r.at[lax.rem(z, 2) * 4 + y], dev)
-        near_copy = pltpu.make_async_copy(src, dst, p_l)
-
-        @pl.when(same)
-        def _():
-            near_copy.start()
-
-        @pl.when(jnp.logical_not(same))
-        def _():
-            far_copy.start()
-        pieces.append((far_copy, near_copy, same))
+
+    def send_cell(k):
+        ys = mod4(y + k)
+        for q in range(4):
+            start = lax.rem(y, 2) * 512 + q * LANES
+            src = na.at[ys, :, pl.ds(pl.multiple_of(start, LANES), LANES)]
+            dst = ao.at[q, z, ys]
+            same = target_self[q]
+            goes = active & jnp.logical_not(same)
+            far_copy = copy(src, dst, p_s.at[k, q], p_r.at[lax.rem(z, 2) * 4 + ys], targets[q])
+            near_copy = pltpu.make_async_copy(src, dst, p_l.at[ys])
+
+            @pl.when(same)
+            def _():
+                near_copy.start()
+
+            @pl.when(goes)
+            def _():
+                far_copy.start()
+            pieces.append((far_copy, goes))
+
+    def wait_pieces():
+        for i, ((zs, ys), same) in enumerate(zip(sources, source_self)):
+            dst = ao.at[x, zs, ys]
+            far_copy = copy(dst, dst, p_s.at[0, 0], p_r.at[i], (z, y, lax.rem(t + 1, 8)))
+            near_copy = pltpu.make_async_copy(dst, dst, p_l.at[ys])
+
+            @pl.when(same)
+            def _():
+                near_copy.wait()
+
+            @pl.when(jnp.logical_not(same))
+            def _():
+                far_copy.wait_recv()
 
     rings = []
 
@@ -156,26 +186,25 @@
             for k in self.go + self.pass_on:
                 k.wait_send()
 
-    even = (pl.ds(0, 96),), (pl.ds(96, 80),)
-    odd = (pl.ds(80, 96),), (pl.ds(0, 80),)
-    equal = (pl.ds(0, 48),), (pl.ds(48, 48),)
+    more_up = (pl.ds(0, 96),), (pl.ds(96, 80),)
+    more_down = (pl.ds(0, 80),), (pl.ds(80, 96),)
 
     def az_ring(k):
         item = mod4(y + k)
-        return Ring(lambda v: ga.at[v, item], "z", *(even if k in (0, 1) else odd))
+        return Ring(lambda v: ga.at[v, item], "z", *(more_up if k in (0, 1) else more_down))
 
     def by_ring(k):
         item = mod4(z + k)
-        return Ring(lambda v: gb.at[v, item], "y", *(even if k in (0, 1) else odd))
+        return Ring(lambda v: gb.at[v, item], "y", *(more_up if k in (0, 1) else more_down))
 
     def rows_of(chunk):
         return pl.ds(pl.multiple_of(chunk * SEG, 8), SEG)
 
-    r_na = Ring(lambda v: na.at[v], "y", *even)
-    r_ca = Ring(lambda v: ca.at[v], "z", *equal)
-    r_cg = Ring(lambda v: cg.at[v], "z", *equal)
-    r_ay = Ring(lambda v: ga.at[z, v], "y", *odd)
-    r_bz = Ring(lambda v: gb.at[y, v], "z", *odd)
+    r_na = Ring(lambda v: na.at[v], "y", *more_up)
+    r_ca = Ring(lambda v: ca.at[v], "z", *more_up)
+    r_cg = Ring(lambda v: cg.at[v], "z", *more_down)
+    r_ay = Ring(lambda v: ga.at[z, v], "y", *more_down)
+    r_bz = Ring(lambda v: gb.at[y, v], "z", *more_down)
     r_az = {k: az_ring(k) for k in (0, 3, 1, 2)}
     r_by = {k: by_ring(k) for k in (0, 3, 1, 2)}
     here = pl.ds(2 * c, 2)
@@ -185,47 +214,37 @@
 
     r_na.start()
     r_ca.start()
-    lax.fori_loop(0, (WA + WB) // LANES, stage_clean, 0)
+    send_cell(0)
+    lax.fori_loop(0, WA // LANES, stage_a, 0)
+    lax.fori_loop(0, HALF // LANES, stage_clean, 0)
     r_cg.start()
-    lax.fori_loop(0, WA // LANES, stage_a, 0)
     lax.fori_loop(0, WB // LANES, stage_b, 0)
 
+    partner = (z, y, 2 * x + 1 - c)
     r_ca.forward()
     r_na.forward()
     r_ay.start()
     r_by[0].start()
-    for i, ((zs, ys), same) in enumerate(zip(sources, source_self)):
-        dst = ao.at[x, zs, ys]
-        far_copy = copy(dst, dst, p_s.at[i], p_r.at[i], (z, y, lax.rem(t + 1, 8)))
-        near_copy = pltpu.make_async_copy(dst, dst, p_l)
-
-        @pl.when(same)
-        def _():
-            near_copy.wait()
-
-        @pl.when(jnp.logical_not(same))
-        def _():
-            far_copy.wait_recv()
-    partner = (z, y, 2 * x + 1 - c)
-    r_ao.start()
-    r_cg.forward()
     r_bz.start()
-    r_az[0].start()
-
-    contract = (((1,), (1,)), ((), ()))
+    send_cell(3)
+    send_cell(1)
 
     def gram(left, right):
-        return lax.dot_general(left, right, contract, preferred_element_type=F32)
+        return lax.dot_general(left, right, (((1,), (1,)), ((), ())), preferred_element_type=F32)
+
+    def unpack(ref, half):
+        part = [ref[v].astype(F32)[half * SEG:(half + 1) * SEG] for v in range(4)]
+        return jnp.concatenate(part, axis=0).astype(BF16)
 
     r_na.finish()
     r_ca.finish()
-    part_gram[...] = gram(na[...].reshape(4 * NOISE, 1024), ca[...].reshape(4 * CLEAN_ROWS, 1024))
+    part_gram[...] = gram(na[:, :, :512].reshape(4 * NOISE, 512), unpack(ca, 0)) + gram(
+        na[:, :, 512:].reshape(4 * NOISE, 512), unpack(ca, 1))
     own_half = pl.ds(pl.multiple_of(c * 352, 8), 352)
     other_half = pl.ds(pl.multiple_of((1 - c) * 352, 8), 352)
     swap = copy(part_gram.at[other_half], d2, d_s.at[0], d_r.at[0], partner)
     swap.start()
-    r_ay.forward()
-
+    send_cell(2)
 
     def turn_a(k):
         def step(q, carry):
@@ -248,6 +267,7 @@
 
     turned = [copy(ata.at[here], ata.at[here], k_s.at[0], k_r.at[0], partner),
               copy(atb.at[c], atb.at[c], k_s.at[1], k_r.at[1], partner)]
+
     swap.wait_recv()
     sm[...] = part_gram[own_half] + d2[...]
     up, down, across = mod4(x + 1), mod4(x + 3), mod4(x + 2)
@@ -260,7 +280,8 @@
              copy(sm.at[rows_of(down)], x3.at[1], m_s.at[3], m_r.at[3], dev_down)]
     share[0].start()
     share[1].start()
-    r_ao.forward()
+    r_ay.forward()
+    r_cg.forward()
     share[0].wait_recv()
     sm[pl.ds(pl.multiple_of(up * SEG, 8), 48)] += near_a[...]
     share[2].start()
@@ -268,28 +289,36 @@
     sm[pl.ds(pl.multiple_of(down * SEG + 48, 8), 40)] += near_b[...]
     share[3].start()
     r_bz.forward()
+    r_az[0].start()
+    r_az[3].start()
+    wait_pieces()
+    r_ao.start()
+    r_by[0].forward()
+    r_by[3].start()
+    r_by[1].start()
+    r_az[1].start()
 
     share[2].wait_recv()
     share[3].wait_recv()
     full[rows_of(4 * c + x)] = sm[rows_of(x)] + x3[0] + x3[1]
     r_full.start()
-    r_by[0].forward()
-    r_by[3].start()
-    r_az[3].start()
+    r_cg.finish()
+    r_ay.finish()
+    r_az[2].start()
     r_full.forward()
+    left[...] = unpack(cg, 0)
+    right[...] = unpack(cg, 1)
+    grad_gram[...] = gram(ga[z].reshape(4 * NOISE, WA), left[:, :WA])
+    r_ao.forward()
     r_full.finish()
     give = copy(full.at[own_half], full.at[own_half], d_s.at[1], d_r.at[1], partner)
     give.start()
-    r_cg.finish()
-    r_ay.finish()
-    grad_gram[...] = gram(ga[z].reshape(4 * NOISE, WA), cg[:, :, :WA].reshape(4 * CLEAN_ROWS, WA))
-    r_ao.finish()
-    turn_a(0)
-    turn_a(1)
-    turned[0].start()
+    r_bz.finish()
+    r_by[2].start()
 
     r_by[0].finish()
-    grad_gram[...] += gram(gb[:, z].reshape(4 * NOISE, WB), cg[:, :, WA:].reshape(4 * CLEAN_ROWS, WB))
+    grad_gram[...] += gram(gb[:, z, :, :HALF - WA].reshape(4 * NOISE, HALF - WA), left[:, WA:]) + gram(
+        gb[:, z, :, HALF - WA:].reshape(4 * NOISE, HALF), right[...])
     copy(full.at[other_half], full.at[other_half], d_s.at[1], d_r.at[1], partner).wait_recv()
 
     def row_dot(j):
@@ -317,19 +346,20 @@
 
     send_tile(sv1, tile, t, 8, lambda r: (z, y, lax.rem(t + r, 8)), 0)
 
-    r_az[0].forward()
+    r_ao.finish()
+    turn_a(0)
+    turn_a(1)
+    turned[0].start()
     tile = sum_tiles(sv1, t, 8, 0)
     send_tile(sv2, tile, 4 * z + y, 16, cell, 8)
-    r_by[1].start()
-    r_az[1].start()
-    r_az[2].start()
-    r_bz.finish()
-    r_by[2].start()
+    r_az[0].forward()
     for v in range(4):
         turn_b(v)
     turned[1].start()
     r_az[3].forward()
     r_by[3].forward()
+    r_az[1].forward()
+    r_by[1].forward()
     tile = sum_tiles(sv2, 4 * z + y, 16, 8)
     weights = jnp.maximum(-tile, 0.0) / jnp.sum(jnp.abs(tile), axis=0, keepdims=True)
     wts[...] = weights
@@ -381,12 +411,10 @@
         product(lambda: jnp.concatenate([atb[0, v], atb[1, v]], axis=1), right_of, WB, WA, first, 512)
 
     add_a(0, True)
-    r_az[1].forward()
-    r_by[1].forward()
     add_b(0, True)
     r_az[2].forward()
+    r_by[2].forward()
     add_a(3)
-    r_by[2].forward()
     add_a(1)
     add_b(3)
     add_b(1)
@@ -397,8 +425,8 @@
         r_by[k].finish()
     add_b(2)
 
-    for far_copy, _, same in pieces:
-        @pl.when(jnp.logical_not(same))
+    for far_copy, goes in pieces:
+        @pl.when(goes)
         def _():
             far_copy.wait_send()
     for ring in rings:
@@ -417,8 +445,10 @@
         out_specs=(pl.BlockSpec(memory_space=pltpu.VMEM), pl.BlockSpec(memory_space=pltpu.VMEM)),
         scratch_shapes=[
             vmem((4, NOISE, 1024), BF16),
-            vmem((4, CLEAN_ROWS, 1024), BF16),
-            vmem((4, CLEAN_ROWS, WA + WB), BF16),
+            vmem((4, NOISE, 512), BF16),
+            vmem((4, NOISE, HALF), BF16),
+            vmem((4 * SEG, HALF), BF16),
+            vmem((4 * SEG, HALF), BF16),
             vmem((4, 4, NOISE, WA), BF16),
             vmem((4, 4, NOISE, WB), BF16),
             vmem((4, 4, 4, NOISE, LANES), BF16),
@@ -436,7 +466,7 @@
             vmem((16, 8, LANES), F32),
             vmem((8, LANES), F32),
             dma((15, 4)), dma((15, 4)),
-            dma((8,)), dma((8,)), dma,
+            dma((4, 4)), dma((8,)), dma((4,)),
             dma((2,)), dma((2,)),
             dma((2,)), dma((2,)),
             dma((4,)), dma((4,)),

time: 98.8 us -> 85.9 us (0.87)
  Pallas kernels: 95.1 us -> 81.7 us
    pallas_call x1, Pallas kernels: 95.1 us -> 81.7 us  [body(): pl.pallas_call(body_kernel, out_shape=(pltpu.VMEM((512, WA + WB), F32), p...]
where the time goes in v11:
time: 85.9 us; the launch traced here: 84.7 us
  Pallas kernels  81.7 us (95%)
  local copies, waits for them, and re-layouts  2.35 us (3%)
    pallas_call x1, Pallas kernels, body(): pl.pallas_call(body_kernel, out_shape=(pltpu.VMEM((512, WA + WB), F32), p...  81.7 us
    unnamed x2, local copies, waits for them, and re-layouts  2.35 us

profile of v11, /device:TPU:0, one launch (start us, length us, event | category | flops | bytes accessed | tf_op | source)
XLA Modules:
  0.0 84.7 jit_solution(793761123395395141)
XLA Ops:
  0.6 81.7 %reweight.1 = (f32[512,1792]{1,0:T(8,128)S(1)}, f32[1,2]{1,0:T(1,128)S(1)}) custom-call(s32[1,3]{1,0:T(1,128)} %ids_ref.1, s32[1,3]{1,0:T(1,128)} %counts_ref.1, bf16[3,88,1024]{2,1,0:T(8,128)(2,1)} %acts_ref.1, bf16[3,88,1792]{2,1,0:T(8,128)(2,1)} %cot_ref.1), custom_call_target="tpu_custom_call" | custom-call | flops 8000000000 | bytes 8000000 | tf_op jit(solution)/shard_map/reweight/pallas_call | solution.py:441
  82.3 1.8 %copy.8 = f32[512,1792]{1,0:T(8,128)} copy(f32[512,1792]{1,0:T(8,128)S(1)} %get-tuple-element.2) | data formatting | bytes 7340032
  84.2 0.5 copy.9

commit v12 on v11

--- a/solution.py
+++ b/solution.py
@@ -200,7 +200,7 @@
     def rows_of(chunk):
         return pl.ds(pl.multiple_of(chunk * SEG, 8), SEG)
 
-    r_na = Ring(lambda v: na.at[v], "y", *more_up)
+    r_na = [Ring(lambda v, h=h: na.at[v, :, pl.ds(h * 512, 512)], "y", *(more_up, more_down)[h]) for h in range(2)]
     r_ca = Ring(lambda v: ca.at[v], "z", *more_up)
     r_cg = Ring(lambda v: cg.at[v], "z", *more_down)
     r_ay = Ring(lambda v: ga.at[z, v], "y", *more_down)
@@ -212,7 +212,8 @@
     r_ao = Ring(lambda v: ao.at[v, here], "x", (pl.ds(0, 1),), (pl.ds(1, 1),))
     r_full = Ring(lambda v: full.at[rows_of(4 * c + v)], "x", (pl.ds(0, 48),), (pl.ds(48, 40),))
 
-    r_na.start()
+    for ring in r_na:
+        ring.start()
     r_ca.start()
     send_cell(0)
     lax.fori_loop(0, WA // LANES, stage_a, 0)
@@ -222,7 +223,8 @@
 
     partner = (z, y, 2 * x + 1 - c)
     r_ca.forward()
-    r_na.forward()
+    for ring in r_na:
+        ring.forward()
     r_ay.start()
     r_by[0].start()
     r_bz.start()
@@ -236,7 +238,8 @@
         part = [ref[v].astype(F32)[half * SEG:(half + 1) * SEG] for v in range(4)]
         return jnp.concatenate(part, axis=0).astype(BF16)
 
-    r_na.finish()
+    for ring in r_na:
+        ring.finish()
     r_ca.finish()
     part_gram[...] = gram(na[:, :, :512].reshape(4 * NOISE, 512), unpack(ca, 0)) + gram(
         na[:, :, 512:].reshape(4 * NOISE, 512), unpack(ca, 1))
@@ -435,10 +438,19 @@
         k.wait_send()
 
 
+def store_kernel(held_ref, weights_ref, out_ref, wout_ref, sems):
+    copies = [pltpu.make_async_copy(held_ref, out_ref, sems.at[0]),
+              pltpu.make_async_copy(weights_ref, wout_ref, sems.at[1])]
+    for k in copies:
+        k.start()
+    for k in copies:
+        k.wait()
+
+
 def body(activations, cotangents, row_ids, row_counts):
     dma = pltpu.SemaphoreType.DMA
     vmem = pltpu.VMEM
-    return pl.pallas_call(
+    held, weights = pl.pallas_call(
         body_kernel,
         out_shape=(pltpu.VMEM((512, WA + WB), F32), pltpu.VMEM((1, 2), F32)),
         in_specs=[pl.BlockSpec(memory_space=pltpu.SMEM)] * 2 + [pl.BlockSpec(memory_space=pltpu.VMEM)] * 2,
@@ -465,7 +477,7 @@
             vmem((8, 8, LANES), F32),
             vmem((16, 8, LANES), F32),
             vmem((8, LANES), F32),
-            dma((15, 4)), dma((15, 4)),
+            dma((16, 4)), dma((16, 4)),
             dma((4, 4)), dma((8,)), dma((4,)),
             dma((2,)), dma((2,)),
             dma((2,)), dma((2,)),
@@ -477,6 +489,14 @@
         cost_estimate=pl.CostEstimate(flops=8_000_000_000, bytes_accessed=8_000_000, transcendentals=0),
         name="reweight",
     )(row_ids, row_counts, activations, cotangents)
+    return pl.pallas_call(
+        store_kernel,
+        out_shape=(jax.ShapeDtypeStruct((512, WA + WB), F32), jax.ShapeDtypeStruct((1, 2), F32)),
+        in_specs=[pl.BlockSpec(memory_space=pltpu.VMEM)] * 2,
+        out_specs=(pl.BlockSpec(memory_space=pl.ANY), pl.BlockSpec(memory_space=pl.ANY)),
+        scratch_shapes=[dma((2,))],
+        name="store",
+    )(held, weights)
 
 
 def solution(mesh):

time: 85.9 us -> 88.6 us (1.031)
  Pallas kernels: 81.7 us -> 85.1 us
    pallas_call x0 -> x1, Pallas kernels: none -> 3.89 us  [body(): pl.pallas_call(store_kernel, out_shape=(jax.ShapeDtypeStruct((512, WA + W...]
    unnamed x2 -> x4, local copies, waits for them, and re-layouts: 2.35 us -> 2.3 us
where the time goes in v12:
time: 88.6 us; the launch traced here: 88.1 us
  Pallas kernels  85.1 us (96%)
  local copies, waits for them, and re-layouts  2.3 us (3%)
    pallas_call x1, Pallas kernels, body(): pl.pallas_call(body_kernel, out_shape=(pltpu.VMEM((512, WA + WB), F32), p...  81.2 us
    pallas_call x1, Pallas kernels, body(): pl.pallas_call(store_kernel, out_shape=(jax.ShapeDtypeStruct((512, WA + W...  3.89 us
    unnamed x4, local copies, waits for them, and re-layouts  2.3 us

profile of v12, /device:TPU:0, one launch (start us, length us, event | category | flops | bytes accessed | tf_op | source)
XLA Modules:
  0.0 88.1 jit_solution(10340064864534084603)
XLA Ops:
  0.6 81.2 %reweight.1 = (f32[512,1792]{1,0:T(8,128)S(1)}, f32[1,2]{1,0:T(1,128)S(1)}) custom-call(s32[1,3]{1,0:T(1,128)} %ids_ref.1, s32[1,3]{1,0:T(1,128)} %counts_ref.1, bf16[3,88,1024]{2,1,0:T(8,128)(2,1)} %acts_ref.1, bf16[3,88,1792]{2,1,0:T(8,128)(2,1)} %cot_ref.1), custom_call_target="tpu_custom_call" | custom-call | flops 8000000000 | bytes 8000000 | tf_op jit(solution)/shard_map/reweight/pallas_call | solution.py:453
  81.9 0.0 copy-start
  81.9 1.8 %copy-done = f32[512,1792]{1,0:T(8,128)} copy-done((f32[512,1792]{1,0:T(8,128)}, f32[512,1792]{1,0:T(8,128)S(1)}, u32[]{:S(2)}) %copy-start) | copy-done | bytes 3670040
  83.7 0.0 copy-start.1
  83.7 0.5 copy-done.1
  84.2 3.9 %store.1 = (f32[512,1792]{1,0:T(8,128)}, f32[1,2]{1,0:T(1,128)}) custom-call(f32[512,1792]{1,0:T(8,128)} %copy-done, f32[1,2]{1,0:T(1,128)} %copy-done.1), custom_call_target="tpu_custom_call" | custom-call | tf_op jit(solution)/shard_map/store/pallas_call | solution.py:492
Async XLA Ops:
  81.9 1.8 %copy-start = (f32[512,1792]{1,0:T(8,128)}, f32[512,1792]{1,0:T(8,128)S(1)}, u32[]{:S(2)}) copy-start(f32[512,1792]{1,0:T(8,128)S(1)} %get-tuple-element.4.held_ref) | copy-start | bytes 11010052
  83.7 0.5 copy-start.1

commit v13 on v11

--- a/solution.py
+++ b/solution.py
@@ -200,7 +200,7 @@
     def rows_of(chunk):
         return pl.ds(pl.multiple_of(chunk * SEG, 8), SEG)
 
-    r_na = Ring(lambda v: na.at[v], "y", *more_up)
+    r_na = [Ring(lambda v, h=h: na.at[v, :, pl.ds(h * 512, 512)], "y", *(more_up, more_down)[h]) for h in range(2)]
     r_ca = Ring(lambda v: ca.at[v], "z", *more_up)
     r_cg = Ring(lambda v: cg.at[v], "z", *more_down)
     r_ay = Ring(lambda v: ga.at[z, v], "y", *more_down)
@@ -212,7 +212,8 @@
     r_ao = Ring(lambda v: ao.at[v, here], "x", (pl.ds(0, 1),), (pl.ds(1, 1),))
     r_full = Ring(lambda v: full.at[rows_of(4 * c + v)], "x", (pl.ds(0, 48),), (pl.ds(48, 40),))
 
-    r_na.start()
+    for ring in r_na:
+        ring.start()
     r_ca.start()
     send_cell(0)
     lax.fori_loop(0, WA // LANES, stage_a, 0)
@@ -222,7 +223,8 @@
 
     partner = (z, y, 2 * x + 1 - c)
     r_ca.forward()
-    r_na.forward()
+    for ring in r_na:
+        ring.forward()
     r_ay.start()
     r_by[0].start()
     r_bz.start()
@@ -236,7 +238,8 @@
         part = [ref[v].astype(F32)[half * SEG:(half + 1) * SEG] for v in range(4)]
         return jnp.concatenate(part, axis=0).astype(BF16)
 
-    r_na.finish()
+    for ring in r_na:
+        ring.finish()
     r_ca.finish()
     part_gram[...] = gram(na[:, :, :512].reshape(4 * NOISE, 512), unpack(ca, 0)) + gram(
         na[:, :, 512:].reshape(4 * NOISE, 512), unpack(ca, 1))
@@ -246,15 +249,17 @@
     swap.start()
     send_cell(2)
 
+    gap = jnp.zeros((32, LANES), BF16)
+
     def turn_a(k):
         def step(q, carry):
             span = pl.ds(pl.multiple_of(q * LANES, LANES), LANES)
-            ata[2 * c + k, span, :] = ao[q, 2 * c + k].reshape(4 * NOISE, LANES).T
+            for g in range(2):
+                cells = [ao[q, 2 * c + k, 2 * g], ao[q, 2 * c + k, 2 * g + 1], gap]
+                ata[2 * c + k, g, span, :] = jnp.concatenate(cells, axis=0).T
             return carry
 
         lax.fori_loop(0, 4, step, 0)
-
-    gap = jnp.zeros((32, LANES), BF16)
 
     def turn_b(v):
         def step(q, carry):
@@ -379,11 +384,18 @@
 
         return jnp.concatenate([part(0), part(1)], axis=0).astype(BF16)
 
-    def product(left_of, right_of, width, base, first, span):
+    def product(lefts, rights, width, base, span, first=False):
+        empty = jnp.zeros((32, span), BF16)
+
         def step(i, carry):
             cols = pl.ds(pl.multiple_of(i * span, span), span)
             dest = pl.ds(pl.multiple_of(base + i * span, 256), span)
-            value = jnp.dot(left_of(), right_of(cols), preferred_element_type=F32)
+            right = []
+            for two in rights:
+                right += [scaled(rows_in[cell_at + (slice(None), cols)].astype(F32), k)
+                          for rows_in, cell_at, k in two] + [empty]
+            left_side = jnp.concatenate([ref[at] for ref, at in lefts], axis=1)
+            value = jnp.dot(left_side, jnp.concatenate(right, axis=0), preferred_element_type=F32)
             if first:
                 out_ref[:, dest] = value
             else:
@@ -392,23 +404,15 @@
 
         lax.fori_loop(0, width // span, step, 0)
 
-    def add_a(k, first=False):
+    def add_a(k, first=False, parts=(0, 1)):
         v = mod4(z + k)
-
-        def right_of(cols):
-            return jnp.concatenate([scaled(ga[v, i, :, cols].astype(F32), v) for i in range(4)], axis=0)
-
-        product(lambda: ata[v], right_of, WA, 0, first, 768)
-
-    def add_b(k, first=False):
+        product([(ata, (v, g)) for g in parts],
+                [[(ga, (v, 2 * g + j), v) for j in range(2)] for g in parts], WA, 0, 768, first)
+
+    def add_b(k, first=False, parts=(0, 1)):
         v = mod4(y + k)
-
-        def right_of(cols):
-            parts = [scaled(gb[v, i, :, cols].astype(F32), i) for i in range(4)]
-            empty = jnp.zeros((32, 512), BF16)
-            return jnp.concatenate([parts[0], parts[1], empty, parts[2], parts[3], empty], axis=0)
-
-        product(lambda: jnp.concatenate([atb[0, v], atb[1, v]], axis=1), right_of, WB, WA, first, 512)
+        product([(atb, (g, v)) for g in parts],
+                [[(gb, (v, 2 * g + j), 2 * g + j) for j in range(2)] for g in parts], WB, WA, 512, first)
 
     add_a(0, True)
     add_b(0, True)
@@ -418,12 +422,16 @@
     add_a(1)
     add_b(3)
     add_b(1)
-    for k in (0, 3, 1, 2):
+    for k in (0, 3, 1):
         r_az[k].finish()
-    add_a(2)
-    for k in (3, 1, 2):
+    add_a(2, parts=(y // 2,))
+    for k in (3, 1):
         r_by[k].finish()
-    add_b(2)
+    add_b(2, parts=(z // 2,))
+    r_az[2].finish()
+    add_a(2, parts=(1 - y // 2,))
+    r_by[2].finish()
+    add_b(2, parts=(1 - z // 2,))
 
     for far_copy, goes in pieces:
         @pl.when(goes)
@@ -452,7 +460,7 @@
             vmem((4, 4, NOISE, WA), BF16),
             vmem((4, 4, NOISE, WB), BF16),
             vmem((4, 4, 4, NOISE, LANES), BF16),
-            vmem((4, 512, 4 * NOISE), BF16),
+            vmem((4, 2, 512, 384), BF16),
             vmem((2, 4, 512, 384), BF16),
             vmem((4 * NOISE, 4 * CLEAN_ROWS), F32),
             vmem((4 * NOISE, 4 * CLEAN_ROWS), F32),
@@ -465,7 +473,7 @@
             vmem((8, 8, LANES), F32),
             vmem((16, 8, LANES), F32),
             vmem((8, LANES), F32),
-            dma((15, 4)), dma((15, 4)),
+            dma((16, 4)), dma((16, 4)),
             dma((4, 4)), dma((8,)), dma((4,)),
             dma((2,)), dma((2,)),
             dma((2,)), dma((2,)),

time: 85.9 us -> 84.4 us (0.983)
  no operation moved by 1% of the time
where the time goes in v13:
time: 84.4 us; the launch traced here: 83.9 us
  Pallas kernels  80.9 us (96%)
  local copies, waits for them, and re-layouts  2.35 us (3%)
    pallas_call x1, Pallas kernels, body(): pl.pallas_call(body_kernel, out_shape=(pltpu.VMEM((512, WA + WB), F32), p...  80.9 us
    unnamed x2, local copies, waits for them, and re-layouts  2.35 us

profile of v13, /device:TPU:0, one launch (start us, length us, event | category | flops | bytes accessed | tf_op | source)
XLA Modules:
  0.0 83.9 jit_solution(15013238504657576353)
XLA Ops:
  0.6 80.9 %reweight.1 = (f32[512,1792]{1,0:T(8,128)S(1)}, f32[1,2]{1,0:T(1,128)S(1)}) custom-call(s32[1,3]{1,0:T(1,128)} %ids_ref.1, s32[1,3]{1,0:T(1,128)} %counts_ref.1, bf16[3,88,1024]{2,1,0:T(8,128)(2,1)} %acts_ref.1, bf16[3,88,1792]{2,1,0:T(8,128)(2,1)} %cot_ref.1), custom_call_target="tpu_custom_call" | custom-call | flops 8000000000 | bytes 8000000 | tf_op jit(solution)/shard_map/reweight/pallas_call | solution.py:449
  81.6 1.8 %copy.8 = f32[512,1792]{1,0:T(8,128)} copy(f32[512,1792]{1,0:T(8,128)S(1)} %get-tuple-element.2) | data formatting | bytes 7340032
  83.4 0.5 copy.9

commit v14 on v13

--- a/solution.py
+++ b/solution.py
@@ -402,17 +402,17 @@
                 out_ref[:, dest] += value
             return carry
 
-        lax.fori_loop(0, width // span, step, 0)
+        lax.fori_loop(0, width // span, step, 0, unroll=True)
 
     def add_a(k, first=False, parts=(0, 1)):
         v = mod4(z + k)
         product([(ata, (v, g)) for g in parts],
-                [[(ga, (v, 2 * g + j), v) for j in range(2)] for g in parts], WA, 0, 768, first)
+                [[(ga, (v, 2 * g + j), v) for j in range(2)] for g in parts], WA, 0, 256, first)
 
     def add_b(k, first=False, parts=(0, 1)):
         v = mod4(y + k)
         product([(atb, (g, v)) for g in parts],
-                [[(gb, (v, 2 * g + j), 2 * g + j) for j in range(2)] for g in parts], WB, WA, 512, first)
+                [[(gb, (v, 2 * g + j), 2 * g + j) for j in range(2)] for g in parts], WB, WA, 256, first)
 
     add_a(0, True)
     add_b(0, True)

time: 84.4 us -> 84.7 us (level)
  no operation moved by 1% of the time
where the time goes in v14:
time: 84.7 us; the launch traced here: 83.8 us
  Pallas kernels  80.8 us (95%)
  local copies, waits for them, and re-layouts  2.35 us (3%)
    pallas_call x1, Pallas kernels, body(): pl.pallas_call(body_kernel, out_shape=(pltpu.VMEM((512, WA + WB), F32), p...  80.8 us
    unnamed x2, local copies, waits for them, and re-layouts  2.35 us

profile of v14, /device:TPU:0, one launch (start us, length us, event | category | flops | bytes accessed | tf_op | source)
XLA Modules:
  0.0 83.8 jit_solution(9844437184127444726)
XLA Ops:
  0.6 80.8 %reweight.1 = (f32[512,1792]{1,0:T(8,128)S(1)}, f32[1,2]{1,0:T(1,128)S(1)}) custom-call(s32[1,3]{1,0:T(1,128)} %ids_ref.1, s32[1,3]{1,0:T(1,128)} %counts_ref.1, bf16[3,88,1024]{2,1,0:T(8,128)(2,1)} %acts_ref.1, bf16[3,88,1792]{2,1,0:T(8,128)(2,1)} %cot_ref.1), custom_call_target="tpu_custom_call" | custom-call | flops 8000000000 | bytes 8000000 | tf_op jit(solution)/shard_map/reweight/pallas_call | solution.py:449
  81.4 1.8 %copy.8 = f32[512,1792]{1,0:T(8,128)} copy(f32[512,1792]{1,0:T(8,128)S(1)} %get-tuple-element.2) | data formatting | bytes 7340032
  83.3 0.5 copy.9

commit v15 on v14

--- a/solution.py
+++ b/solution.py
@@ -131,10 +131,12 @@
                 far_copy.start()
             pieces.append((far_copy, goes))
 
-    def wait_pieces():
-        for i, ((zs, ys), same) in enumerate(zip(sources, source_self)):
-            dst = ao.at[x, zs, ys]
-            far_copy = copy(dst, dst, p_s.at[0, 0], p_r.at[i], (z, y, lax.rem(t + 1, 8)))
+    def wait_pieces(k):
+        ys = mod4(y + k)
+        for j in range(2):
+            dst = ao.at[x, 2 * c + j, ys]
+            same = active & (x == z) & (2 * c + j == z)
+            far_copy = copy(dst, dst, p_s.at[0, 0], p_r.at[4 * j + ys], (z, y, lax.rem(t + 1, 8)))
             near_copy = pltpu.make_async_copy(dst, dst, p_l.at[ys])
 
             @pl.when(same)
@@ -209,7 +211,11 @@
     r_by = {k: by_ring(k) for k in (0, 3, 1, 2)}
     here = pl.ds(2 * c, 2)
     there = pl.ds(2 * (1 - c), 2)
-    r_ao = Ring(lambda v: ao.at[v, here], "x", (pl.ds(0, 1),), (pl.ds(1, 1),))
+
+    def ao_ring(k):
+        return Ring(lambda v: ao.at[v, here, mod4(y + k)], "x", (pl.ds(0, 1),), (pl.ds(1, 1),))
+
+    r_ao = {k: ao_ring(k) for k in (0, 3, 1, 2)}
     r_full = Ring(lambda v: full.at[rows_of(4 * c + v)], "x", (pl.ds(0, 48),), (pl.ds(48, 40),))
 
     for ring in r_na:
@@ -227,9 +233,11 @@
         ring.forward()
     r_ay.start()
     r_by[0].start()
-    r_bz.start()
     send_cell(3)
     send_cell(1)
+    r_bz.start()
+    wait_pieces(0)
+    r_ao[0].start()
 
     def gram(left, right):
         return lax.dot_general(left, right, (((1,), (1,)), ((), ())), preferred_element_type=F32)
@@ -248,6 +256,10 @@
     swap = copy(part_gram.at[other_half], d2, d_s.at[0], d_r.at[0], partner)
     swap.start()
     send_cell(2)
+    r_ao[0].forward()
+    for k in (3, 1):
+        wait_pieces(k)
+        r_ao[k].start()
 
     gap = jnp.zeros((32, LANES), BF16)
 
@@ -296,8 +308,8 @@
     r_bz.forward()
     r_az[0].start()
     r_az[3].start()
-    wait_pieces()
-    r_ao.start()
+    r_ao[3].forward()
+    r_ao[1].forward()
     r_by[0].forward()
     r_by[3].start()
     r_by[1].start()
@@ -311,13 +323,15 @@
     r_ay.finish()
     r_az[2].start()
     r_full.forward()
+    wait_pieces(2)
+    r_ao[2].start()
     left[...] = unpack(cg, 0)
     right[...] = unpack(cg, 1)
     grad_gram[...] = gram(ga[z].reshape(4 * NOISE, WA), left[:, :WA])
-    r_ao.forward()
     r_full.finish()
     give = copy(full.at[own_half], full.at[own_half], d_s.at[1], d_r.at[1], partner)
     give.start()
+    r_ao[2].forward()
     r_bz.finish()
     r_by[2].start()
 
@@ -351,7 +365,8 @@
 
     send_tile(sv1, tile, t, 8, lambda r: (z, y, lax.rem(t + r, 8)), 0)
 
-    r_ao.finish()
+    for k in (0, 3, 1, 2):
+        r_ao[k].finish()
     turn_a(0)
     turn_a(1)
     turned[0].start()
@@ -473,7 +488,7 @@
             vmem((8, 8, LANES), F32),
             vmem((16, 8, LANES), F32),
             vmem((8, LANES), F32),
-            dma((16, 4)), dma((16, 4)),
+            dma((19, 4)), dma((19, 4)),
             dma((4, 4)), dma((8,)), dma((4,)),
             dma((2,)), dma((2,)),
             dma((2,)), dma((2,)),

time: 84.7 us -> 85 us (level)
  Pallas kernels: 80.8 us -> 81.9 us
    pallas_call x1, Pallas kernels: 80.8 us -> 81.9 us  [body(): pl.pallas_call(body_kernel, out_shape=(pltpu.VMEM((512, WA + WB), F32), p...]
where the time goes in v15:
time: 85 us; the launch traced here: 84.9 us
  Pallas kernels  81.9 us (96%)
  local copies, waits for them, and re-layouts  2.35 us (3%)
    pallas_call x1, Pallas kernels, body(): pl.pallas_call(body_kernel, out_shape=(pltpu.VMEM((512, WA + WB), F32), p...  81.9 us
    unnamed x2, local copies, waits for them, and re-layouts  2.35 us

profile of v15, /device:TPU:0, one launch (start us, length us, event | category | flops | bytes accessed | tf_op | source)
XLA Modules:
  0.0 84.9 jit_solution(8247658137254303043)
XLA Ops:
  0.6 81.9 %reweight.1 = (f32[512,1792]{1,0:T(8,128)S(1)}, f32[1,2]{1,0:T(1,128)S(1)}) custom-call(s32[1,3]{1,0:T(1,128)} %ids_ref.1, s32[1,3]{1,0:T(1,128)} %counts_ref.1, bf16[3,88,1024]{2,1,0:T(8,128)(2,1)} %acts_ref.1, bf16[3,88,1792]{2,1,0:T(8,128)(2,1)} %cot_ref.1), custom_call_target="tpu_custom_call" | custom-call | flops 8000000000 | bytes 8000000 | tf_op jit(solution)/shard_map/reweight/pallas_call | solution.py:464
  82.5 1.8 %copy.8 = f32[512,1792]{1,0:T(8,128)} copy(f32[512,1792]{1,0:T(8,128)S(1)} %get-tuple-element.2) | data formatting | bytes 7340032
  84.4 0.5 copy.9

commit v16 on v15

--- a/solution.py
+++ b/solution.py
@@ -365,29 +365,25 @@
 
     send_tile(sv1, tile, t, 8, lambda r: (z, y, lax.rem(t + r, 8)), 0)
 
+    tile = sum_tiles(sv1, t, 8, 0)
+    send_tile(sv2, tile, 4 * z + y, 16, cell, 8)
+    r_az[0].forward()
     for k in (0, 3, 1, 2):
         r_ao[k].finish()
     turn_a(0)
     turn_a(1)
     turned[0].start()
-    tile = sum_tiles(sv1, t, 8, 0)
-    send_tile(sv2, tile, 4 * z + y, 16, cell, 8)
-    r_az[0].forward()
     for v in range(4):
         turn_b(v)
     turned[1].start()
     r_az[3].forward()
     r_by[3].forward()
-    r_az[1].forward()
-    r_by[1].forward()
     tile = sum_tiles(sv2, 4 * z + y, 16, 8)
     weights = jnp.maximum(-tile, 0.0) / jnp.sum(jnp.abs(tile), axis=0, keepdims=True)
     wts[...] = weights
     lane = lax.broadcasted_iota(jnp.int32, (1, LANES), 1)
     wout_ref[...] = jnp.where(lane == 0, wts[pl.ds(2 * z, 1), :], wts[pl.ds(2 * z + 1, 1), :])[:, :2]
 
-    copy(ata.at[there], ata.at[there], k_s.at[0], k_r.at[0], partner).wait_recv()
-    copy(atb.at[1 - c], atb.at[1 - c], k_s.at[1], k_r.at[1], partner).wait_recv()
 
     def scaled(rows_in, k):
         width = rows_in.shape[1]
@@ -429,11 +425,15 @@
         product([(atb, (g, v)) for g in parts],
                 [[(gb, (v, 2 * g + j), 2 * g + j) for j in range(2)] for g in parts], WB, WA, 256, first)
 
+    copy(ata.at[there], ata.at[there], k_s.at[0], k_r.at[0], partner).wait_recv()
     add_a(0, True)
+    r_az[1].forward()
+    r_by[1].forward()
+    copy(atb.at[1 - c], atb.at[1 - c], k_s.at[1], k_r.at[1], partner).wait_recv()
     add_b(0, True)
     r_az[2].forward()
+    add_a(3)
     r_by[2].forward()
-    add_a(3)
     add_a(1)
     add_b(3)
     add_b(1)

time: 85 us -> 85.2 us (level)
  no operation moved by 1% of the time
where the time goes in v16:
time: 85.2 us; the launch traced here: 85.1 us
  Pallas kernels  82.1 us (96%)
  local copies, waits for them, and re-layouts  2.35 us (3%)
    pallas_call x1, Pallas kernels, body(): pl.pallas_call(body_kernel, out_shape=(pltpu.VMEM((512, WA + WB), F32), p...  82.1 us
    unnamed x2, local copies, waits for them, and re-layouts  2.35 us

profile of v16, /device:TPU:0, one launch (start us, length us, event | category | flops | bytes accessed | tf_op | source)
XLA Modules:
  0.0 85.1 jit_solution(979492341122944798)
XLA Ops:
  0.6 82.1 %reweight.1 = (f32[512,1792]{1,0:T(8,128)S(1)}, f32[1,2]{1,0:T(1,128)S(1)}) custom-call(s32[1,3]{1,0:T(1,128)} %ids_ref.1, s32[1,3]{1,0:T(1,128)} %counts_ref.1, bf16[3,88,1024]{2,1,0:T(8,128)(2,1)} %acts_ref.1, bf16[3,88,1792]{2,1,0:T(8,128)(2,1)} %cot_ref.1), custom_call_target="tpu_custom_call" | custom-call | flops 8000000000 | bytes 8000000 | tf_op jit(solution)/shard_map/reweight/pallas_call | solution.py:464
  82.7 1.8 %copy.8 = f32[512,1792]{1,0:T(8,128)} copy(f32[512,1792]{1,0:T(8,128)S(1)} %get-tuple-element.2) | data formatting | bytes 7340032
  84.6 0.5 copy.9

commit v17 on v13

--- a/solution.py
+++ b/solution.py
@@ -248,6 +248,7 @@
     swap = copy(part_gram.at[other_half], d2, d_s.at[0], d_r.at[0], partner)
     swap.start()
     send_cell(2)
+    r_az[0].start()
 
     gap = jnp.zeros((32, LANES), BF16)
 
@@ -294,7 +295,6 @@
     sm[pl.ds(pl.multiple_of(down * SEG + 48, 8), 40)] += near_b[...]
     share[3].start()
     r_bz.forward()
-    r_az[0].start()
     r_az[3].start()
     wait_pieces()
     r_ao.start()

time: 84.4 us -> 85.1 us (level)
  no operation moved by 1% of the time
where the time goes in v17:
time: 85.1 us; the launch traced here: 84.1 us
  Pallas kernels  81.1 us (95%)
  local copies, waits for them, and re-layouts  2.35 us (3%)
    pallas_call x1, Pallas kernels, body(): pl.pallas_call(body_kernel, out_shape=(pltpu.VMEM((512, WA + WB), F32), p...  81.1 us
    unnamed x2, local copies, waits for them, and re-layouts  2.35 us

profile of v17, /device:TPU:0, one launch (start us, length us, event | category | flops | bytes accessed | tf_op | source)
XLA Modules:
  0.0 84.1 jit_solution(7010577437759206622)
XLA Ops:
  0.6 81.1 %reweight.1 = (f32[512,1792]{1,0:T(8,128)S(1)}, f32[1,2]{1,0:T(1,128)S(1)}) custom-call(s32[1,3]{1,0:T(1,128)} %ids_ref.1, s32[1,3]{1,0:T(1,128)} %counts_ref.1, bf16[3,88,1024]{2,1,0:T(8,128)(2,1)} %acts_ref.1, bf16[3,88,1792]{2,1,0:T(8,128)(2,1)} %cot_ref.1), custom_call_target="tpu_custom_call" | custom-call | flops 8000000000 | bytes 8000000 | tf_op jit(solution)/shard_map/reweight/pallas_call | solution.py:449
  81.7 1.8 %copy.8 = f32[512,1792]{1,0:T(8,128)} copy(f32[512,1792]{1,0:T(8,128)S(1)} %get-tuple-element.2) | data formatting | bytes 7340032
  83.6 0.5 copy.9
